TPU v7x, 32 devices: a whole 2x2x4 slice. The times are simulated.
32 devices in a mesh: grp: 4 (over x, core), box: 8 (over z, y).
Axes of the slice: x: 2, y: 2, z: 4, core: 2. Of those that a mesh axis runs over, the one named last changes fastest.
Arguments:
- right_side: float32 [64, 256, 128], P('grp', 'box'), may hold values from -6 to 6
- beta: float32 [64, 256, 128], P('grp', 'box'), may hold values from 0.25 to 4
Outputs:
- correction: float32 [64, 256, 128], P('grp', 'box')
All inputs are finite; a program needn't handle non-finite values.
Results may differ from a plain program's by a relative error of at most 0.0001.
Values sent between devices are 32-bit elements; how exact they have to be, the bound alone decides.
A program may use at most 64 MiB of HBM per device.

v0:
```python
import functools

import jax
import jax.numpy as jnp
from jax import lax
from jax.experimental import pallas as pl
from jax.experimental.pallas import tpu as pltpu
from jax.sharding import PartitionSpec as P

LEVELS = 4
SWEEPS = 2
COARSE = 8
W = 2.0 / 3.0
MESH = pl.DeviceIdType.MESH
F32 = jnp.float32

X0, Y0, LANES = 16, 32, 128
H0 = 4
H1 = 5
HY = 8
DIRS = [(dx, dy) for dx in (-1, 0, 1) for dy in (-1, 0, 1) if (dx, dy) != (0, 0)]


def roll(v, shift, axis):
    return pltpu.roll(v, shift % v.shape[axis], axis)


def lane_of(shape):
    return lax.broadcasted_iota(jnp.int32, shape, len(shape) - 1)


def pair_lanes(v, apart):
    lane = lane_of(v.shape)
    return v + jnp.where((lane & apart) == 0, roll(v, -apart, 1), roll(v, apart, 1))


def span(size, halo, step, own):
    if step == 0:
        return (halo, size), (halo, size)
    if step < 0:
        return (halo, own), (halo + size, own)
    return (halo + size - own, own), (halo - own, own)


def kernel(
    G, B, rs_ref, be_ref, out_ref,
    B0, S0, V0, U0, CX0, CY0, CM0, CP0, Q0, D0,
    B1, S1, V1, U1, CX1, CY1, CM1, CP1, Q1, D1,
    T, PB, PS, GB, GS, V2, C2, C3, C4, E, F3,
    halo_send, halo_recv, ga_send, ga_recv, rounds, loc_sem,
):
    n = G * B
    g = lax.axis_index("grp")
    b = lax.axis_index("box")
    me = g * B + b
    ry2, ry3, ry4 = 8 * B, 4 * B, 2 * B

    own0 = (pl.ds(H0, X0), pl.ds(HY, Y0))
    load_b = pltpu.make_async_copy(be_ref, B0.at[own0[0], own0[1]], loc_sem.at[0])
    load_s = pltpu.make_async_copy(rs_ref, S0.at[own0[0], own0[1]], loc_sem.at[1])
    load_b.start()
    load_s.start()

    barrier = pltpu.get_barrier_semaphore()

    partners = []
    step = 1
    while step < G:
        partners.append((step, (g + step * (1 - 2 * ((g // step) % 2)), b)))
        step *= 2
    step = 1
    while step < B:
        partners.append((step, (g, b + step * (1 - 2 * ((b // step) % 2)))))
        step *= 2
    expected = 0
    for dx, dy in DIRS:
        there = (g + dx >= 0) & (g + dx < G) & (b + dy >= 0) & (b + dy < B)
        expected = expected + there.astype(jnp.int32)

        @pl.when(there)
        def _():
            pl.semaphore_signal(barrier, inc=1, device_id=(g + dx, b + dy), device_id_type=MESH)

    for step, partner in partners:
        if step > 1:
            expected = expected + 1
            pl.semaphore_signal(barrier, inc=1, device_id=partner, device_id_type=MESH)

    def tell(k):
        pl.semaphore_signal(rounds.at[k], inc=1, device_id=partners[k][1], device_id_type=MESH)

    def hear(k):
        pl.semaphore_wait(rounds.at[k], 1)

    for ref, nx, hx, ny in ((B0, X0, H0, Y0), (S0, X0, H0, Y0), (B1, X0 // 2, H1, Y0 // 2), (S1, X0 // 2, H1, Y0 // 2)):
        rows = ny + 2 * HY
        planes = nx + 2 * hx

        @pl.when(g == 0)
        def _():
            ref[pl.ds(0, hx)] = jnp.zeros((hx, rows, LANES), F32)

        @pl.when(g == G - 1)
        def _():
            ref[pl.ds(hx + nx, hx)] = jnp.zeros((hx, rows, LANES), F32)

        @pl.when(b == 0)
        def _():
            ref[:, pl.ds(0, HY)] = jnp.zeros((planes, HY, LANES), F32)

        @pl.when(b == B - 1)
        def _():
            ref[:, pl.ds(HY + ny, HY)] = jnp.zeros((planes, HY, LANES), F32)

    V2[0] = jnp.zeros((ry2 + 16, LANES), F32)
    V2[G + 1] = jnp.zeros((ry2 + 16, LANES), F32)
    V2[:, pl.ds(0, 8)] = jnp.zeros((G + 2, 8, LANES), F32)
    V2[:, pl.ds(8 + ry2, 8)] = jnp.zeros((G + 2, 8, LANES), F32)

    pl.semaphore_wait(barrier, expected)

    def halo_copies(kind, src, dst, nx, hx, ny, deep, corner, tall, src_is_input):
        made = []
        for at, (dx, dy) in enumerate(DIRS):
            (sx, lx), (tx, _) = span(nx, hx, dx, deep if dy == 0 else corner)
            (sy, ly), (ty, _) = span(ny, HY, dy, tall)
            if src_is_input:
                sx, sy = sx - hx, sy - HY
            copy = pltpu.make_async_remote_copy(
                src_ref=src.at[pl.ds(sx, lx), pl.ds(sy, ly)],
                dst_ref=dst.at[pl.ds(tx, lx), pl.ds(ty, ly)],
                send_sem=halo_send.at[kind, at],
                recv_sem=halo_recv.at[kind, at],
                device_id=(g + dx, b + dy),
                device_id_type=MESH,
            )
            there = (g + dx >= 0) & (g + dx < G) & (b + dy >= 0) & (b + dy < B)
            here = (g - dx >= 0) & (g - dx < G) & (b - dy >= 0) & (b - dy < B)
            made.append((copy, there, here))
        return made

    def start_all(copies):
        for copy, there, _ in copies:
            pl.when(there)(copy.start)

    def recv_all(copies):
        for copy, _, here in copies:
            pl.when(here)(copy.wait_recv)

    def sent_all(copies):
        for copy, there, _ in copies:
            pl.when(there)(copy.wait_send)

    def gather_start(which, packed, whole):
        pltpu.make_async_copy(packed, whole.at[g, pl.ds(pl.multiple_of(b * 8, 8), 8)], ga_recv.at[which]).start()

        def one(d, carry):
            peer = (me + d) % n
            pltpu.make_async_remote_copy(
                src_ref=packed,
                dst_ref=whole.at[g, pl.ds(pl.multiple_of(b * 8, 8), 8)],
                send_sem=ga_send.at[which, d],
                recv_sem=ga_recv.at[which],
                device_id=(peer // B, peer % B),
                device_id_type=MESH,
            ).start()
            return carry

        lax.fori_loop(1, n, one, 0, unroll=True)

    def gather_recv(which, whole):
        pltpu.make_async_copy(whole, whole, ga_recv.at[which]).wait()

    def gather_sent(which, packed):
        def one(d, carry):
            pltpu.make_async_copy(packed, packed, ga_send.at[which, d]).wait()
            return carry

        lax.fori_loop(1, n, one, 0, unroll=True)

    beta_halo = halo_copies(0, be_ref, B0, X0, H0, Y0, 4, 3, 4, True)
    source_halo = halo_copies(1, rs_ref, S0, X0, H0, Y0, 3, 2, 4, True)
    start_all(beta_halo)
    start_all(source_halo)
    tell(0)
    load_b.wait()

    def halve(pair, apart, slot):
        rows = pair.shape[0]
        T[slot, pl.ds(0, rows)] = pair_lanes(pair, apart)
        return 0.125 * (T[slot, pl.ds(0, rows // 2, stride=2)] + T[slot, pl.ds(1, rows // 2, stride=2)])

    def pack(planes):
        lane = lane_of(planes[0].shape) & 3
        packed = planes[3]
        for k in (2, 1, 0):
            packed = jnp.where(lane == k, planes[k], packed)
        return packed

    for p in range(X0 // 2):
        B1[H1 + p, pl.ds(HY, Y0 // 2)] = halve(
            B0[H0 + 2 * p, pl.ds(HY, Y0)] + B0[H0 + 2 * p + 1, pl.ds(HY, Y0)], 1, p
        )
    beta1_halo = halo_copies(2, B1, B1, X0 // 2, H1, Y0 // 2, 5, 5, 8, False)
    PB[...] = pack([
        halve(B1[H1 + 2 * p, pl.ds(HY, Y0 // 2)] + B1[H1 + 2 * p + 1, pl.ds(HY, Y0 // 2)], 2, p)
        for p in range(X0 // 4)
    ])

    def setup(level, Bl, CX, CY, CM, CP, Q, D, first, last, row, rows, hx, nx, ny):
        apart = 1 << level
        h = 0.5 * 0.25**level

        def plane(i, carry):
            at = pl.ds(row, rows)
            c = Bl[i, at]
            xm = Bl[i - 1, at]
            xp = Bl[i + 1, at]
            ym = Bl[i, pl.ds(row - 1, rows)]
            yp = Bl[i, pl.ds(row + 1, rows)]
            lane = lane_of(c.shape)
            low = lane >= apart
            high = lane < LANES - apart
            zm = jnp.where(low, roll(c, apart, 1), 0.0)
            zp = jnp.where(high, roll(c, -apart, 1), 0.0)
            CX[i, at] = h * (c + xm)
            CY[i, at] = h * (c + ym)
            CM[i, at] = jnp.where(low, h * (c + zm), 0.0)
            CP[i, at] = jnp.where(high, h * (c + zp), 0.0)
            d = h * (6.0 * c + ((xm + xp) + (ym + yp) + (zm + zp)))
            D[i, at] = d
            x = g * nx + i - hx
            y = lax.broadcasted_iota(jnp.int32, c.shape, 0) + (b * ny + row - HY)
            inside = (y >= 0) & (y < B * ny) & (x >= 0) & (x < G * nx)
            Q[i, at] = jnp.where(inside, W / d, 0.0)
            return carry

        lax.fori_loop(first, last, plane, 0, unroll=True)

    def across(level, V, CX, CY, CM, CP, i, row, rows):
        apart = 1 << level
        at = pl.ds(row, rows)
        up = pl.ds(row + 1, rows)
        v = V[i, at]
        total = CX[i, at] * V[i - 1, at] + CX[i + 1, at] * V[i + 1, at]
        total = total + (CY[i, at] * V[i, pl.ds(row - 1, rows)] + CY[i, up] * V[i, up])
        total = total + (CM[i, at] * roll(v, apart, 1) + CP[i, at] * roll(v, -apart, 1))
        return v, total

    def first_sweep(V, Q, S, first, last, row, rows):
        def plane(i, carry):
            V[i, pl.ds(row, rows)] = Q[i, pl.ds(row, rows)] * S[i, pl.ds(row, rows)]
            return carry

        lax.fori_loop(first, last, plane, 0, unroll=True)

    def sweep(level, V, U, S, Q, coeffs, first, last, row, rows, drop_x=0, drop_y=0):
        def plane(i, carry):
            v, total = across(level, V, *coeffs, i, row, rows)
            U[i - drop_x, pl.ds(row - drop_y, rows)] = (1.0 - W) * v + Q[i, pl.ds(row, rows)] * (
                S[i, pl.ds(row, rows)] + total
            )
            return carry

        lax.fori_loop(first, last, plane, 0, unroll=True)

    def residual(level, V, S, D, coeffs, i, row, rows):
        v, total = across(level, V, *coeffs, i, row, rows)
        return S[i, pl.ds(row, rows)] - (D[i, pl.ds(row, rows)] * v - total)

    coeffs0 = (CX0, CY0, CM0, CP0)
    coeffs1 = (CX1, CY1, CM1, CP1)
    row0, rows0 = 4, 40
    row1, rows1 = 4, 24

    hear(0)
    tell(1)
    recv_all(beta_halo)
    hear(1)
    tell(2)
    setup(0, B0, CX0, CY0, CM0, CP0, Q0, D0, 1, 23, row0, rows0, H0, X0, Y0)
    load_s.wait()
    recv_all(source_halo)
    start_all(beta1_halo)
    hear(2)
    tell(3)
    first_sweep(V0, Q0, S0, 1, 23, row0, rows0)
    sweep(0, V0, U0, S0, Q0, coeffs0, 2, 22, row0, rows0)

    hear(3)
    tell(4)
    for k in range(5, len(partners)):
        hear(k - 1)
        tell(k)

    def down0(p, carry):
        i = H0 + 2 * p
        pair = residual(0, U0, S0, D0, coeffs0, i, HY, Y0) + residual(0, U0, S0, D0, coeffs0, i + 1, HY, Y0)
        S1[H1 + p, pl.ds(HY, Y0 // 2)] = halve(pair, 1, p)
        return carry

    lax.fori_loop(0, X0 // 2, down0, 0, unroll=True)
    source1_halo = halo_copies(3, S1, S1, X0 // 2, H1, Y0 // 2, 4, 4, 4, False)
    start_all(source1_halo)
    hear(len(partners) - 1)
    gather_start(0, PB, GB)

    recv_all(beta1_halo)
    setup(1, B1, CX1, CY1, CM1, CP1, Q1, D1, 1, 17, row1, rows1, H1, X0 // 2, Y0 // 2)
    recv_all(source1_halo)
    first_sweep(V1, Q1, S1, 1, 17, row1, rows1)
    sweep(1, V1, U1, S1, Q1, coeffs1, 2, 16, row1, rows1)
    planes = []
    for p in range(X0 // 4):
        i = H1 + 2 * p
        pair = residual(1, U1, S1, D1, coeffs1, i, HY, Y0 // 2) + residual(1, U1, S1, D1, coeffs1, i + 1, HY, Y0 // 2)
        planes.append(halve(pair, 2, p))
    PS[...] = pack(planes)
    gather_start(1, PS, GS)

    def neighbours(v, level):
        st, zs = 1 << (level - 2), 1 << level
        before = [v[i - 1] for i in range(G)]
        after = [v[(i + 1) % G] for i in range(G)]
        if st == 4:
            xm, xp = before, after
        else:
            k = lane_of(v[0].shape) & 3
            xm = [jnp.where(k >= st, roll(v[i], st, 1), roll(before[i], st - 4, 1)) for i in range(G)]
            xp = [jnp.where(k < 4 - st, roll(v[i], -st, 1), roll(after[i], 4 - st, 1)) for i in range(G)]
        ym = [roll(a, 1, 0) for a in v]
        yp = [roll(a, -1, 0) for a in v]
        zm = [roll(a, zs, 1) for a in v]
        zp = [roll(a, -zs, 1) for a in v]
        return xm, xp, ym, yp, zm, zp

    def setup_whole(beta, C, level):
        st, zs = 1 << (level - 2), 1 << level
        h = 0.5 * 0.25**level
        near = neighbours(beta, level)
        shape = beta[0].shape
        lane = lane_of(shape)
        row = lax.broadcasted_iota(jnp.int32, shape, 0)
        for i in range(G):
            ok = [
                ((lane & 3) >= st) if i == 0 else None,
                ((lane & 3) < 4 - st) if i == G - 1 else None,
                row > 0,
                row < shape[0] - 1,
                lane >= zs,
                lane < LANES - zs,
            ]
            total = 6.0 * beta[i]
            for d in range(6):
                there = near[d][i] if ok[d] is None else jnp.where(ok[d], near[d][i], 0.0)
                total = total + there
                face = h * (beta[i] + there)
                C[d, i] = face if ok[d] is None else jnp.where(ok[d], face, 0.0)
            diag = h * total
            C[6, i] = diag
            C[7, i] = W / diag

    def sum_across(v, C, level):
        near = neighbours(v, level)
        out = []
        for i in range(G):
            out.append(
                (C[0, i] * near[0][i] + C[1, i] * near[1][i])
                + (C[2, i] * near[2][i] + C[3, i] * near[3][i])
                + (C[4, i] * near[4][i] + C[5, i] * near[5][i])
            )
        return out

    def sweep_whole(v, s, C, level):
        total = sum_across(v, C, level)
        return [(1.0 - W) * v[i] + C[7, i] * (s[i] + total[i]) for i in range(G)]

    def coarsen(v, level):
        st, zs = 1 << (level - 2), 1 << level
        rows = v[0].shape[0]
        out = []
        for i in range(G):
            E[i, pl.ds(0, rows)] = pair_lanes(pair_lanes(v[i], st), zs)
            out.append(0.125 * (E[i, pl.ds(0, rows // 2, stride=2)] + E[i, pl.ds(1, rows // 2, stride=2)]))
        return out

    def refine(v):
        rows = v[0].shape[0]
        out = []
        for i in range(G):
            E[i, pl.ds(0, rows, stride=2)] = v[i]
            E[i, pl.ds(1, rows, stride=2)] = v[i]
            out.append(E[i, pl.ds(0, 2 * rows)])
        return out

    gather_recv(0, GB)
    beta2 = [GB[i] for i in range(G)]
    setup_whole(beta2, C2, 2)
    beta3 = coarsen(beta2, 2)
    setup_whole(beta3, C3, 3)
    beta4 = coarsen(beta3, 3)
    setup_whole(beta4, C4, 4)

    gather_recv(1, GS)
    s2 = [GS[i] for i in range(G)]
    v = [C2[7, i] * s2[i] for i in range(G)]
    v = sweep_whole(v, s2, C2, 2)
    for i in range(G):
        V2[i + 1, pl.ds(8, ry2)] = v[i]
    total = sum_across(v, C2, 2)
    s3 = coarsen([s2[i] - (C2[6, i] * v[i] - total[i]) for i in range(G)], 2)
    v = [C3[7, i] * s3[i] for i in range(G)]
    v = sweep_whole(v, s3, C3, 3)
    for i in range(G):
        F3[0, i] = v[i]
        F3[1, i] = s3[i]
    total = sum_across(v, C3, 3)
    s4 = coarsen([s3[i] - (C3[6, i] * v[i] - total[i]) for i in range(G)], 3)

    def dot(a, c):
        acc = a[0] * c[0]
        for i in range(1, G):
            acc = acc + a[i] * c[i]
        part = acc[0:8]
        for j in range(8, ry4, 8):
            part = part + acc[j : j + 8]
        return jnp.sum(jnp.sum(part, axis=0, keepdims=True), axis=1, keepdims=True)

    def cg(step, carry):
        x, r, p, rr = carry
        near = sum_across(p, C4, 4)
        q = [C4[6, i] * p[i] - near[i] for i in range(G)]
        alpha = rr / dot(p, q)
        x = [x[i] + alpha * p[i] for i in range(G)]
        r = [r[i] - alpha * q[i] for i in range(G)]
        new = dot(r, r)
        ratio = new / rr
        p = [r[i] + ratio * p[i] for i in range(G)]
        return x, r, p, new

    zero = [jnp.zeros((ry4, LANES), F32) for i in range(G)]
    x4 = lax.fori_loop(0, COARSE, cg, (zero, s4, s4, dot(s4, s4)), unroll=True)[0]

    up = refine(x4)
    s3 = [F3[1, i] for i in range(G)]
    v = [F3[0, i] + up[i] for i in range(G)]
    for _ in range(SWEEPS):
        v = sweep_whole(v, s3, C3, 3)
    up = refine(v)
    s2 = [GS[i] for i in range(G)]
    v = [V2[i + 1, pl.ds(8, ry2)] + up[i] for i in range(G)]
    for _ in range(SWEEPS):
        v = sweep_whole(v, s2, C2, 2)
    for i in range(G):
        V2[i + 1, pl.ds(8, ry2)] = v[i]

    for x2 in range(-2, 6):
        k = x2 % 4
        window = V2[g + 1 + x2 // 4, pl.ds(pl.multiple_of(b * 8, 8), 24)]
        one = jnp.where((lane_of(window.shape) & 3) == k, window, 0.0)
        one = one + roll(one, 1 if k in (0, 2) else -1, 1)
        one = one + roll(one, 2 if k in (0, 1) else -2, 1)
        T[x2 + 2, pl.ds(0, 24)] = one
    for x2 in range(-2, 6):
        add = T[x2 + 2, pl.ds(6, 12)]
        for i in (2 * x2 + 5, 2 * x2 + 6):
            if 2 <= i < 16:
                for odd in (0, 1):
                    at = pl.ds(row1 + odd, 12, stride=2)
                    U1[i, at] = U1[i, at] + add
    sweep(1, U1, V1, S1, Q1, coeffs1, 3, 15, row1, rows1)
    sweep(1, V1, U1, S1, Q1, coeffs1, 4, 14, row1, rows1)

    def prolong0(i, carry):
        add = U1[i + 3, pl.ds(6, 20)]
        for half in (0, 1):
            for odd in (0, 1):
                at = pl.ds(row0 + odd, 20, stride=2)
                U0[2 * i + half, at] = U0[2 * i + half, at] + add
        return carry

    lax.fori_loop(1, 11, prolong0, 0, unroll=True)
    sweep(0, U0, V0, S0, Q0, coeffs0, 3, 21, row0, rows0)
    sweep(0, V0, out_ref, S0, Q0, coeffs0, 4, 20, HY, Y0, H0, HY)

    sent_all(beta_halo)
    sent_all(source_halo)
    sent_all(beta1_halo)
    sent_all(source1_halo)
    gather_sent(0, PB)
    gather_sent(1, PS)


def in_one_kernel(G, B, right_side, beta):
    level0 = pltpu.VMEM((X0 + 2 * H0, Y0 + 2 * HY, LANES), F32)
    level1 = pltpu.VMEM((X0 // 2 + 2 * H1, Y0 // 2 + 2 * HY, LANES), F32)
    return pl.pallas_call(
        functools.partial(kernel, G, B),
        out_shape=jax.ShapeDtypeStruct(right_side.shape, F32),
        in_specs=[pl.BlockSpec(memory_space=pl.ANY)] * 2,
        out_specs=pl.BlockSpec(memory_space=pltpu.VMEM),
        scratch_shapes=[level0] * 10
        + [level1] * 10
        + [
            pltpu.VMEM((8, Y0, LANES), F32),
            pltpu.VMEM((8, LANES), F32),
            pltpu.VMEM((8, LANES), F32),
            pltpu.VMEM((G, 8 * B, LANES), F32),
            pltpu.VMEM((G, 8 * B, LANES), F32),
            pltpu.VMEM((G + 2, 8 * B + 16, LANES), F32),
            pltpu.VMEM((8, G, 8 * B, LANES), F32),
            pltpu.VMEM((8, G, 4 * B, LANES), F32),
            pltpu.VMEM((8, G, 2 * B, LANES), F32),
            pltpu.VMEM((G, 8 * B, LANES), F32),
            pltpu.VMEM((2, G, 4 * B, LANES), F32),
            pltpu.SemaphoreType.DMA((4, 8)),
            pltpu.SemaphoreType.DMA((4, 8)),
            pltpu.SemaphoreType.DMA((2, G * B)),
            pltpu.SemaphoreType.DMA((2,)),
            pltpu.SemaphoreType.REGULAR((8,)),
            pltpu.SemaphoreType.DMA((2,)),
        ],
        compiler_params=pltpu.CompilerParams(
            collective_id=0, has_side_effects=True, vmem_limit_bytes=40 * 1024 * 1024
        ),
    )(right_side, beta)


relax_weight = 2.0 / 3.0


def with_halo(shard, sides, width):
    for axis, dim in sides:
        size, length = (lax.axis_size(axis), shard.shape[dim])
        up = [(i, (i + 1) % size) for i in range(size - 1)]
        down = [(j, i) for i, j in up]
        last = lax.slice_in_dim(shard, length - width, length, axis=dim)
        leading = lax.slice_in_dim(shard, 0, width, axis=dim)
        before = lax.ppermute(last, axis, up)
        after = lax.ppermute(leading, axis, down)
        shard = jnp.concatenate([before, shard, after], axis=dim)
    return shard


def from_partner(block, axis, apart):
    count = lax.axis_size(axis)
    route = []
    for low in range(count):
        high = low | 1 << apart
        if high != low and high < count:
            route += [(low, high), (high, low)]
    return lax.ppermute(block, axis, route)


def pad_zeros(field):
    return jnp.pad(field, 1)


def pad_local(field):
    extended = with_halo(field, (("grp", 0), ("box", 1)), 1)
    return jnp.pad(extended, ((0, 0), (0, 0), (1, 1)))


def face_coeffs(padded_beta):
    face_x = 0.5 * (padded_beta[1:, 1:-1, 1:-1] + padded_beta[:-1, 1:-1, 1:-1])
    face_y = 0.5 * (padded_beta[1:-1, 1:, 1:-1] + padded_beta[1:-1, :-1, 1:-1])
    face_z = 0.5 * (padded_beta[1:-1, 1:-1, 1:] + padded_beta[1:-1, 1:-1, :-1])
    return (face_x, face_y, face_z)


def inverse_diagonal(coeffs, scale):
    face_x, face_y, face_z = coeffs
    total = (
        face_x[:-1]
        + face_x[1:]
        + face_y[:, :-1]
        + face_y[:, 1:]
        + face_z[:, :, :-1]
        + face_z[:, :, 1:]
    )
    return 1.0 / (scale * total)


def apply_operator(padded, coeffs, scale):
    face_x, face_y, face_z = coeffs
    centre = padded[1:-1, 1:-1, 1:-1]
    total = face_x[:-1] * (centre - padded[:-2, 1:-1, 1:-1]) + face_x[1:] * (
        centre - padded[2:, 1:-1, 1:-1]
    )
    total = (
        total
        + face_y[:, :-1] * (centre - padded[1:-1, :-2, 1:-1])
        + face_y[:, 1:] * (centre - padded[1:-1, 2:, 1:-1])
    )
    total = (
        total
        + face_z[:, :, :-1] * (centre - padded[1:-1, 1:-1, :-2])
        + face_z[:, :, 1:] * (centre - padded[1:-1, 1:-1, 2:])
    )
    return scale * total


def jacobi_sweeps(field, source, coeffs, inverse, scale, count, padder):
    for sweep_index in range(count):
        field = (
            field + relax_weight * (source - apply_operator(padder(field), coeffs, scale)) * inverse
        )
    return field


def conjugate_solve(source, coeffs, scale, count):
    field = jnp.zeros_like(source)
    remain = source
    direction = source
    norm_now = jnp.sum(remain * remain)
    for step_index in range(count):
        image = apply_operator(pad_zeros(direction), coeffs, scale)
        alpha = norm_now / jnp.sum(direction * image)
        field = field + alpha * direction
        remain = remain - alpha * image
        norm_next = jnp.sum(remain * remain)
        direction = remain + norm_next / norm_now * direction
        norm_now = norm_next
    return field


def restrict_mean(field):
    size_a, size_b, size_c = field.shape
    blocks = field.reshape(size_a // 2, 2, size_b // 2, 2, size_c // 2, 2)
    return jnp.mean(blocks, axis=(1, 3, 5))


def prolong_copy(field):
    return jnp.repeat(jnp.repeat(jnp.repeat(field, 2, axis=0), 2, axis=1), 2, axis=2)


def merge_groups(pieces):
    group_index = lax.axis_index("grp")
    for bit_index in range(lax.axis_size("grp").bit_length() - 1):
        partner = from_partner(pieces, "grp", bit_index)
        upper = group_index >> bit_index & 1 == 1
        pieces = tuple(
            (
                jnp.where(
                    upper,
                    jnp.concatenate([theirs, own_piece], 0),
                    jnp.concatenate([own_piece, theirs], 0),
                )
                for own_piece, theirs in zip(pieces, partner)
            )
        )
    return pieces


def merge_boxes(pieces):
    return lax.all_gather(pieces, "box", axis=1, tiled=True)


def shards(right_side, beta):
    source = right_side
    level_beta = beta
    saved = []
    for level in range(LEVELS):
        scale = 0.25**level
        coeffs = face_coeffs(pad_local(level_beta))
        inverse = inverse_diagonal(coeffs, scale)
        field = relax_weight * source * inverse
        field = jacobi_sweeps(field, source, coeffs, inverse, scale, SWEEPS - 1, pad_local)
        residual = source - apply_operator(pad_local(field), coeffs, scale)
        saved.append((field, source, coeffs, inverse, scale))
        source = restrict_mean(residual)
        level_beta = restrict_mean(level_beta)
    low_scale = 0.25**LEVELS
    whole_source, whole_beta = merge_boxes(merge_groups((source, level_beta)))
    low_coeffs = face_coeffs(pad_zeros(whole_beta))
    whole_field = conjugate_solve(whole_source, low_coeffs, low_scale, COARSE)
    block_a, block_b, block_c = source.shape
    field = lax.dynamic_slice(
        whole_field,
        (lax.axis_index("grp") * block_a, lax.axis_index("box") * block_b, 0),
        (block_a, block_b, block_c),
    )
    for level in range(LEVELS - 1, -1, -1):
        kept, level_source, coeffs, inverse, scale = saved[level]
        field = kept + prolong_copy(field)
        field = jacobi_sweeps(field, level_source, coeffs, inverse, scale, SWEEPS, pad_local)
    return field


def solution(mesh):
    placed = P("grp", "box", None)
    G, B = mesh.shape["grp"], mesh.shape["box"]
    small = (G, B) in ((4, 8), (8, 8), (4, 16), (8, 4), (2, 16))

    def local(right_side, beta):
        if small and right_side.shape == (X0, Y0, LANES):
            return in_one_kernel(G, B, right_side, beta)
        return shards(right_side, beta)

    return jax.shard_map(local, mesh=mesh, in_specs=(placed, placed), out_specs=placed, check_vma=False)
```

profile of v0, /device:TPU:0, one launch (start us, length us, event | category | flops | bytes accessed | tf_op | source)
XLA Modules:
  0.0 31.3 jit_solution(16340505403865179097)
XLA Ops:
  0.0 0.0 copy-start
  0.0 0.9 %copy-done = f32[16,32,128]{2,1,0:T(8,128)S(1)} copy-done((f32[16,32,128]{2,1,0:T(8,128)S(1)}, f32[16,32,128]{2,1,0:T(8,128)}, u32[]{:S(2)}) %copy-start) | copy-done | bytes 262168
  1.0 0.0 copy-start.1
  1.0 0.9 %copy-done.1 = f32[16,32,128]{2,1,0:T(8,128)S(1)} copy-done((f32[16,32,128]{2,1,0:T(8,128)S(1)}, f32[16,32,128]{2,1,0:T(8,128)}, u32[]{:S(2)}) %copy-start.1) | copy-done | bytes 262168
  1.9 28.7 %shard_map.28 = f32[16,32,128]{2,1,0:T(8,128)S(1)} custom-call(f32[16,32,128]{2,1,0:T(8,128)S(1)} %copy-done, f32[16,32,128]{2,1,0:T(8,128)S(1)} %copy-done.1), custom_call_target="tpu_custom_call" | custom-call | tf_op jit(solution)/shard_map/pallas_call | solution.py:497
  30.6 0.7 %copy.4 = f32[16,32,128]{2,1,0:T(8,128)} copy(f32[16,32,128]{2,1,0:T(8,128)S(1)} %shard_map.28) | data formatting | bytes 524288
Async XLA Ops:
  0.0 0.9 %copy-start = (f32[16,32,128]{2,1,0:T(8,128)S(1)}, f32[16,32,128]{2,1,0:T(8,128)}, u32[]{:S(2)}) copy-start(f32[16,32,128]{2,1,0:T(8,128)} %rs_ref.1) | copy-start | bytes 786436
  1.0 0.9 %copy-start.1 = (f32[16,32,128]{2,1,0:T(8,128)S(1)}, f32[16,32,128]{2,1,0:T(8,128)}, u32[]{:S(2)}) copy-start(f32[16,32,128]{2,1,0:T(8,128)} %be_ref.1) | copy-start | bytes 786436
where the time goes:
time: 31.5 us; the launch traced here: 31.3 us
  Pallas kernels  28.7 us (91%)
  local copies, waits for them, and re-layouts  2.6 us (8%)
    pallas_call x1, Pallas kernels, in_one_kernel(): pl.pallas_call(functools.partial(kernel, G, B), out_shape=jax.ShapeDtypeS...  28.7 us
    unnamed x5, local copies, waits for them, and re-layouts  2.6 us

commit v1 on v0

--- a/solution.py
+++ b/solution.py
@@ -34,20 +34,20 @@
     return v + jnp.where((lane & apart) == 0, roll(v, -apart, 1), roll(v, apart, 1))
 
 
-def span(size, halo, step, own):
+def span(size, halo, step, near, far):
     if step == 0:
         return (halo, size), (halo, size)
     if step < 0:
-        return (halo, own), (halo + size, own)
-    return (halo + size - own, own), (halo - own, own)
+        return (halo + near, far - near), (halo + size + near, far - near)
+    return (halo + size - far, far - near), (halo - far, far - near)
 
 
 def kernel(
     G, B, rs_ref, be_ref, out_ref,
     B0, S0, V0, U0, CX0, CY0, CM0, CP0, Q0, D0,
     B1, S1, V1, U1, CX1, CY1, CM1, CP1, Q1, D1,
-    T, PB, PS, GB, GS, V2, C2, C3, C4, E, F3,
-    halo_send, halo_recv, ga_send, ga_recv, rounds, loc_sem,
+    T, PB, PS, GB, GS, V2, C2, C3, C4, E, F3, LX0, LY0, LX1, LY1,
+    halo_send, halo_recv, late_send, late_recv, ga_send, ga_recv, rounds, loc_sem,
 ):
     n = G * B
     g = lax.axis_index("grp")
@@ -63,15 +63,6 @@
 
     barrier = pltpu.get_barrier_semaphore()
 
-    partners = []
-    step = 1
-    while step < G:
-        partners.append((step, (g + step * (1 - 2 * ((g // step) % 2)), b)))
-        step *= 2
-    step = 1
-    while step < B:
-        partners.append((step, (g, b + step * (1 - 2 * ((b // step) % 2)))))
-        step *= 2
     expected = 0
     for dx, dy in DIRS:
         there = (g + dx >= 0) & (g + dx < G) & (b + dy >= 0) & (b + dy < B)
@@ -81,16 +72,38 @@
         def _():
             pl.semaphore_signal(barrier, inc=1, device_id=(g + dx, b + dy), device_id_type=MESH)
 
-    for step, partner in partners:
-        if step > 1:
-            expected = expected + 1
-            pl.semaphore_signal(barrier, inc=1, device_id=partner, device_id_type=MESH)
+    reach = max(1, -(-(B - 2) // 3))
+    others = []
+    for far in range(2, G):
+        for dx in (-far, far):
+            others += [(dx, dy) for dy in (-1, 0, 1)]
+    for far in range(2, reach + 1):
+        others += [(0, -far), (0, far)]
+    for dx, dy in others:
+        there = (g + dx >= 0) & (g + dx < G) & (b + dy >= 0) & (b + dy < B)
+        expected = expected + there.astype(jnp.int32)
+
+        @pl.when(there)
+        def _():
+            pl.semaphore_signal(barrier, inc=1, device_id=(g + dx, b + dy), device_id_type=MESH)
+
+    def boxes_of(k):
+        for far in range(k * reach + 1, (k + 1) * reach + 1):
+            for dy in (-far, far):
+                yield b + dy, (b + dy >= 0) & (b + dy < B)
 
     def tell(k):
-        pl.semaphore_signal(rounds.at[k], inc=1, device_id=partners[k][1], device_id_type=MESH)
+        for other, there in boxes_of(k):
+
+            @pl.when(there)
+            def _():
+                pl.semaphore_signal(rounds.at[k], inc=1, device_id=(g, other), device_id_type=MESH)
 
     def hear(k):
-        pl.semaphore_wait(rounds.at[k], 1)
+        count = 0
+        for _, there in boxes_of(k):
+            count = count + there.astype(jnp.int32)
+        pl.semaphore_wait(rounds.at[k], count)
 
     for ref, nx, hx, ny in ((B0, X0, H0, Y0), (S0, X0, H0, Y0), (B1, X0 // 2, H1, Y0 // 2), (S1, X0 // 2, H1, Y0 // 2)):
         rows = ny + 2 * HY
@@ -117,27 +130,82 @@
     V2[:, pl.ds(0, 8)] = jnp.zeros((G + 2, 8, LANES), F32)
     V2[:, pl.ds(8 + ry2, 8)] = jnp.zeros((G + 2, 8, LANES), F32)
 
+    load_b.wait()
+
+    def halve(pair, apart, slot):
+        rows = pair.shape[0]
+        T[slot, pl.ds(0, rows)] = pair_lanes(pair, apart)
+        return 0.125 * (T[slot, pl.ds(0, rows // 2, stride=2)] + T[slot, pl.ds(1, rows // 2, stride=2)])
+
+    def pack(planes):
+        lane = lane_of(planes[0].shape) & 3
+        packed = planes[3]
+        for k in (2, 1, 0):
+            packed = jnp.where(lane == k, planes[k], packed)
+        return packed
+
+    for p in range(X0 // 2):
+        B1[H1 + p, pl.ds(HY, Y0 // 2)] = halve(
+            B0[H0 + 2 * p, pl.ds(HY, Y0)] + B0[H0 + 2 * p + 1, pl.ds(HY, Y0)], 1, p
+        )
+    PB[...] = pack([
+        halve(B1[H1 + 2 * p, pl.ds(HY, Y0 // 2)] + B1[H1 + 2 * p + 1, pl.ds(HY, Y0 // 2)], 2, p)
+        for p in range(X0 // 4)
+    ])
+
+    load_s.wait()
     pl.semaphore_wait(barrier, expected)
 
-    def halo_copies(kind, src, dst, nx, hx, ny, deep, corner, tall, src_is_input):
+    def there_from(dx, dy):
+        return (g + dx >= 0) & (g + dx < G) & (b + dy >= 0) & (b + dy < B)
+
+    def halo_copies(kind, ref, nx, hx, ny, deep, tall, corner):
         made = []
         for at, (dx, dy) in enumerate(DIRS):
-            (sx, lx), (tx, _) = span(nx, hx, dx, deep if dy == 0 else corner)
-            (sy, ly), (ty, _) = span(ny, HY, dy, tall)
-            if src_is_input:
-                sx, sy = sx - hx, sy - HY
+            (sx, lx), (tx, _) = span(nx, hx, dx, 0, deep if dy == 0 else corner)
+            (sy, ly), (ty, _) = span(ny, HY, dy, 0, tall if dx == 0 else corner)
             copy = pltpu.make_async_remote_copy(
-                src_ref=src.at[pl.ds(sx, lx), pl.ds(sy, ly)],
-                dst_ref=dst.at[pl.ds(tx, lx), pl.ds(ty, ly)],
+                src_ref=ref.at[pl.ds(sx, lx), pl.ds(sy, ly)],
+                dst_ref=ref.at[pl.ds(tx, lx), pl.ds(ty, ly)],
                 send_sem=halo_send.at[kind, at],
                 recv_sem=halo_recv.at[kind, at],
                 device_id=(g + dx, b + dy),
                 device_id_type=MESH,
             )
-            there = (g + dx >= 0) & (g + dx < G) & (b + dy >= 0) & (b + dy < B)
-            here = (g - dx >= 0) & (g - dx < G) & (b - dy >= 0) & (b - dy < B)
-            made.append((copy, there, here))
+            made.append((copy, there_from(dx, dy), there_from(-dx, -dy)))
         return made
+
+    def late_copies(kind, ref, LX, LY, nx, hx, ny, near, far):
+        made, land = [], []
+        for at, (dx, dy) in enumerate(((-1, 0), (1, 0), (0, -1), (0, 1))):
+            (sx, lx), (tx, _) = span(nx, hx, dx, near, far)
+            (sy, ly), (ty, _) = span(ny, HY, dy, near, far)
+            box = LX.at[at] if dy == 0 else LY.at[at - 2, :, pl.ds(0, far - near)]
+            copy = pltpu.make_async_remote_copy(
+                src_ref=ref.at[pl.ds(sx, lx), pl.ds(sy, ly)],
+                dst_ref=box,
+                send_sem=late_send.at[kind, at],
+                recv_sem=late_recv.at[kind, at],
+                device_id=(g + dx, b + dy),
+                device_id_type=MESH,
+            )
+            here = there_from(-dx, -dy)
+            made.append((copy, there_from(dx, dy), here))
+
+            def put(tx=tx, lx=lx, ty=ty, ly=ly, box=box):
+                ref[pl.ds(tx, lx), pl.ds(ty, ly)] = box[...]
+
+            land.append((here, put))
+        return made, land
+
+    def land_all(late):
+        made, land = late
+        for (copy, _, here), (_, put) in zip(made, land):
+
+            @pl.when(here)
+            def _():
+                copy.wait_recv()
+                put()
 
     def start_all(copies):
         for copy, there, _ in copies:
@@ -178,34 +246,15 @@
 
         lax.fori_loop(1, n, one, 0, unroll=True)
 
-    beta_halo = halo_copies(0, be_ref, B0, X0, H0, Y0, 4, 3, 4, True)
-    source_halo = halo_copies(1, rs_ref, S0, X0, H0, Y0, 3, 2, 4, True)
+    beta_halo = halo_copies(0, B0, X0, H0, Y0, 3, 3, 3)
+    source_halo = halo_copies(1, S0, X0, H0, Y0, 2, 2, 2)
+    beta1_halo = halo_copies(2, B1, X0 // 2, H1, Y0 // 2, 5, 5, 5)
+    beta_late = late_copies(0, B0, LX0.at[0], LY0.at[0], X0, H0, Y0, 3, 4)
+    source_late = late_copies(1, S0, LX0.at[1], LY0.at[1], X0, H0, Y0, 2, 3)
     start_all(beta_halo)
     start_all(source_halo)
     tell(0)
-    load_b.wait()
-
-    def halve(pair, apart, slot):
-        rows = pair.shape[0]
-        T[slot, pl.ds(0, rows)] = pair_lanes(pair, apart)
-        return 0.125 * (T[slot, pl.ds(0, rows // 2, stride=2)] + T[slot, pl.ds(1, rows // 2, stride=2)])
-
-    def pack(planes):
-        lane = lane_of(planes[0].shape) & 3
-        packed = planes[3]
-        for k in (2, 1, 0):
-            packed = jnp.where(lane == k, planes[k], packed)
-        return packed
-
-    for p in range(X0 // 2):
-        B1[H1 + p, pl.ds(HY, Y0 // 2)] = halve(
-            B0[H0 + 2 * p, pl.ds(HY, Y0)] + B0[H0 + 2 * p + 1, pl.ds(HY, Y0)], 1, p
-        )
-    beta1_halo = halo_copies(2, B1, B1, X0 // 2, H1, Y0 // 2, 5, 5, 8, False)
-    PB[...] = pack([
-        halve(B1[H1 + 2 * p, pl.ds(HY, Y0 // 2)] + B1[H1 + 2 * p + 1, pl.ds(HY, Y0 // 2)], 2, p)
-        for p in range(X0 // 4)
-    ])
+    start_all(beta1_halo)
 
     def setup(level, Bl, CX, CY, CM, CP, Q, D, first, last, row, rows, hx, nx, ny):
         apart = 1 << level
@@ -273,25 +322,13 @@
     row0, rows0 = 4, 40
     row1, rows1 = 4, 24
 
+    recv_all(beta_halo)
     hear(0)
     tell(1)
-    recv_all(beta_halo)
-    hear(1)
-    tell(2)
-    setup(0, B0, CX0, CY0, CM0, CP0, Q0, D0, 1, 23, row0, rows0, H0, X0, Y0)
-    load_s.wait()
+    setup(0, B0, CX0, CY0, CM0, CP0, Q0, D0, 2, 22, row0, rows0, H0, X0, Y0)
     recv_all(source_halo)
-    start_all(beta1_halo)
-    hear(2)
-    tell(3)
-    first_sweep(V0, Q0, S0, 1, 23, row0, rows0)
-    sweep(0, V0, U0, S0, Q0, coeffs0, 2, 22, row0, rows0)
-
-    hear(3)
-    tell(4)
-    for k in range(5, len(partners)):
-        hear(k - 1)
-        tell(k)
+    first_sweep(V0, Q0, S0, 2, 22, row0, rows0)
+    sweep(0, V0, U0, S0, Q0, coeffs0, 3, 21, row0, rows0)
 
     def down0(p, carry):
         i = H0 + 2 * p
@@ -300,16 +337,20 @@
         return carry
 
     lax.fori_loop(0, X0 // 2, down0, 0, unroll=True)
-    source1_halo = halo_copies(3, S1, S1, X0 // 2, H1, Y0 // 2, 4, 4, 4, False)
+    source1_halo = halo_copies(3, S1, X0 // 2, H1, Y0 // 2, 2, 2, 4)
+    source1_late = late_copies(2, S1, LX1, LY1, X0 // 2, H1, Y0 // 2, 2, 4)
     start_all(source1_halo)
-    hear(len(partners) - 1)
+    hear(1)
     gather_start(0, PB, GB)
+    start_all(source1_late[0])
+    start_all(beta_late[0])
+    start_all(source_late[0])
 
     recv_all(beta1_halo)
     setup(1, B1, CX1, CY1, CM1, CP1, Q1, D1, 1, 17, row1, rows1, H1, X0 // 2, Y0 // 2)
     recv_all(source1_halo)
-    first_sweep(V1, Q1, S1, 1, 17, row1, rows1)
-    sweep(1, V1, U1, S1, Q1, coeffs1, 2, 16, row1, rows1)
+    first_sweep(V1, Q1, S1, 3, 15, row1, rows1)
+    sweep(1, V1, U1, S1, Q1, coeffs1, 4, 14, row1, rows1)
     planes = []
     for p in range(X0 // 4):
         i = H1 + 2 * p
@@ -317,6 +358,15 @@
         planes.append(halve(pair, 2, p))
     PS[...] = pack(planes)
     gather_start(1, PS, GS)
+
+    land_all(source1_late)
+    first_sweep(V1, Q1, S1, 1, 17, row1, rows1)
+    sweep(1, V1, U1, S1, Q1, coeffs1, 2, 16, row1, rows1)
+    land_all(beta_late)
+    land_all(source_late)
+    setup(0, B0, CX0, CY0, CM0, CP0, Q0, D0, 1, 23, row0, rows0, H0, X0, Y0)
+    first_sweep(V0, Q0, S0, 1, 23, row0, rows0)
+    sweep(0, V0, U0, S0, Q0, coeffs0, 2, 22, row0, rows0)
 
     def neighbours(v, level):
         st, zs = 1 << (level - 2), 1 << level
@@ -487,6 +537,9 @@
     sent_all(source_halo)
     sent_all(beta1_halo)
     sent_all(source1_halo)
+    sent_all(beta_late[0])
+    sent_all(source_late[0])
+    sent_all(source1_late[0])
     gather_sent(0, PB)
     gather_sent(1, PS)
 
@@ -497,7 +550,7 @@
     return pl.pallas_call(
         functools.partial(kernel, G, B),
         out_shape=jax.ShapeDtypeStruct(right_side.shape, F32),
-        in_specs=[pl.BlockSpec(memory_space=pl.ANY)] * 2,
+        in_specs=[pl.BlockSpec(memory_space=pltpu.HBM)] * 2,
         out_specs=pl.BlockSpec(memory_space=pltpu.VMEM),
         scratch_shapes=[level0] * 10
         + [level1] * 10
@@ -513,8 +566,14 @@
             pltpu.VMEM((8, G, 2 * B, LANES), F32),
             pltpu.VMEM((G, 8 * B, LANES), F32),
             pltpu.VMEM((2, G, 4 * B, LANES), F32),
+            pltpu.VMEM((2, 2, 1, Y0, LANES), F32),
+            pltpu.VMEM((2, 2, X0, 8, LANES), F32),
+            pltpu.VMEM((2, 2, Y0 // 2, LANES), F32),
+            pltpu.VMEM((2, X0 // 2, 8, LANES), F32),
             pltpu.SemaphoreType.DMA((4, 8)),
             pltpu.SemaphoreType.DMA((4, 8)),
+            pltpu.SemaphoreType.DMA((3, 4)),
+            pltpu.SemaphoreType.DMA((3, 4)),
             pltpu.SemaphoreType.DMA((2, G * B)),
             pltpu.SemaphoreType.DMA((2,)),
             pltpu.SemaphoreType.REGULAR((8,)),
@@ -523,7 +582,7 @@
         compiler_params=pltpu.CompilerParams(
             collective_id=0, has_side_effects=True, vmem_limit_bytes=40 * 1024 * 1024
         ),
-    )(right_side, beta)
+    )(*(pltpu.with_memory_space_constraint(a, pltpu.HBM) for a in (right_side, beta)))
 
 
 relax_weight = 2.0 / 3.0

time: 31.5 us -> 28.5 us (0.905)
  local copies, waits for them, and re-layouts: 2.6 us -> 0.71 us
  Pallas kernels: 28.7 us -> 27.6 us
    unnamed x5 -> x1, local copies, waits for them, and re-layouts: 2.6 us -> 0.71 us
    pallas_call x1, Pallas kernels: 28.7 us -> 27.6 us  [in_one_kernel(): pl.pallas_call(functools.partial(kernel, G, B), out_shape=jax.ShapeDtypeS...]
where the time goes in v1:
time: 28.5 us; the launch traced here: 28.3 us
  Pallas kernels  27.6 us (97%)
  local copies, waits for them, and re-layouts  0.71 us (2%)
    pallas_call x1, Pallas kernels, in_one_kernel(): pl.pallas_call(functools.partial(kernel, G, B), out_shape=jax.ShapeDtypeS...  27.6 us
    unnamed x1, local copies, waits for them, and re-layouts  0.71 us

profile of v1, /device:TPU:0, one launch (start us, length us, event | category | flops | bytes accessed | tf_op | source)
XLA Modules:
  0.0 28.3 jit_solution(5064980780431629437)
XLA Ops:
  0.0 27.6 %shard_map.28 = f32[16,32,128]{2,1,0:T(8,128)S(1)} custom-call(f32[16,32,128]{2,1,0:T(8,128)} %rs_ref.1, f32[16,32,128]{2,1,0:T(8,128)} %be_ref.1), custom_call_target="tpu_custom_call" | custom-call | tf_op jit(solution)/shard_map/pallas_call | solution.py:550
  27.6 0.7 %copy.4 = f32[16,32,128]{2,1,0:T(8,128)} copy(f32[16,32,128]{2,1,0:T(8,128)S(1)} %shard_map.28) | data formatting | bytes 524288

commit v2 on v1

--- a/solution.py
+++ b/solution.py
@@ -46,8 +46,8 @@
     G, B, rs_ref, be_ref, out_ref,
     B0, S0, V0, U0, CX0, CY0, CM0, CP0, Q0, D0,
     B1, S1, V1, U1, CX1, CY1, CM1, CP1, Q1, D1,
-    T, PB, PS, GB, GS, V2, C2, C3, C4, E, F3, LX0, LY0, LX1, LY1,
-    halo_send, halo_recv, late_send, late_recv, ga_send, ga_recv, rounds, loc_sem,
+    T, SZ1, PB, PS, P3, PG, GB, GS, GE, V2, Z2, C2, C3, C4, E, E2, F, F3, LX0, LY0, LX1, LY1,
+    halo_send, halo_recv, late_send, late_recv, win_send, win_recv, ga_send, ga_recv, rounds, loc_sem,
 ):
     n = G * B
     g = lax.axis_index("grp")
@@ -125,10 +125,21 @@
         def _():
             ref[:, pl.ds(HY + ny, HY)] = jnp.zeros((planes, HY, LANES), F32)
 
-    V2[0] = jnp.zeros((ry2 + 16, LANES), F32)
-    V2[G + 1] = jnp.zeros((ry2 + 16, LANES), F32)
-    V2[:, pl.ds(0, 8)] = jnp.zeros((G + 2, 8, LANES), F32)
-    V2[:, pl.ds(8 + ry2, 8)] = jnp.zeros((G + 2, 8, LANES), F32)
+    for ref in (SZ1, V1, U1, V2, Z2):
+        ref[...] = jnp.zeros(ref.shape, F32)
+    for side, edge in ((0, 0), (16, B - 1)):
+        for ref in (GB, GS):
+
+            @pl.when(b == edge)
+            def _():
+                ref[:, pl.ds(side, 8)] = jnp.zeros((G, 8, LANES), F32)
+
+    E2[:, pl.ds(0, 8)] = jnp.zeros((G, 8, LANES), F32)
+    E2[:, pl.ds(8 + ry2, 8)] = jnp.zeros((G, 8, LANES), F32)
+    F[0] = jnp.zeros((8, LANES), F32)
+    F[G + 1] = jnp.zeros((8, LANES), F32)
+    GE[:, :, pl.ds(0, 8)] = jnp.zeros((2, G, 8, LANES), F32)
+    GE[:, :, pl.ds(8 + ry3, 8)] = jnp.zeros((2, G, 8, LANES), F32)
 
     load_b.wait()
 
@@ -152,6 +163,10 @@
         halve(B1[H1 + 2 * p, pl.ds(HY, Y0 // 2)] + B1[H1 + 2 * p + 1, pl.ds(HY, Y0 // 2)], 2, p)
         for p in range(X0 // 4)
     ])
+    GB[g, pl.ds(8, 8)] = PB[...]
+    T[0, pl.ds(0, 8)] = pair_lanes(pair_lanes(PB[...], 1), 4)
+    P3[...] = jnp.zeros((8, LANES), F32)
+    P3[pl.ds(2, 4)] = 0.125 * (T[0, pl.ds(0, 4, stride=2)] + T[0, pl.ds(1, 4, stride=2)])
 
     load_s.wait()
     pl.semaphore_wait(barrier, expected)
@@ -219,16 +234,35 @@
         for copy, there, _ in copies:
             pl.when(there)(copy.wait_send)
 
-    def gather_start(which, packed, whole):
-        pltpu.make_async_copy(packed, whole.at[g, pl.ds(pl.multiple_of(b * 8, 8), 8)], ga_recv.at[which]).start()
+    def window_copies(kind, packed, whole):
+        made = []
+        for o in range(G):
+            for dy in (-1, 0, 1):
+                if (o, dy) == (0, 0):
+                    continue
+                at = 3 * o + dy + 1
+                copy = pltpu.make_async_remote_copy(
+                    src_ref=packed,
+                    dst_ref=whole.at[g, pl.ds(8 - 8 * dy, 8)],
+                    send_sem=win_send.at[kind, at],
+                    recv_sem=win_recv.at[kind, at],
+                    device_id=((g + o) % G, b + dy),
+                    device_id_type=MESH,
+                )
+                made.append((copy, (b + dy >= 0) & (b + dy < B), (b - dy >= 0) & (b - dy < B)))
+        return made
+
+    def gather_start():
+        spot = GE.at[b % 2, g, pl.ds(pl.multiple_of(8 + 8 * (b // 2), 8), 8)]
+        pltpu.make_async_copy(PG, spot, ga_recv.at[0]).start()
 
         def one(d, carry):
             peer = (me + d) % n
             pltpu.make_async_remote_copy(
-                src_ref=packed,
-                dst_ref=whole.at[g, pl.ds(pl.multiple_of(b * 8, 8), 8)],
-                send_sem=ga_send.at[which, d],
-                recv_sem=ga_recv.at[which],
+                src_ref=PG,
+                dst_ref=spot,
+                send_sem=ga_send.at[d],
+                recv_sem=ga_recv.at[0],
                 device_id=(peer // B, peer % B),
                 device_id_type=MESH,
             ).start()
@@ -236,12 +270,13 @@
 
         lax.fori_loop(1, n, one, 0, unroll=True)
 
-    def gather_recv(which, whole):
-        pltpu.make_async_copy(whole, whole, ga_recv.at[which]).wait()
-
-    def gather_sent(which, packed):
+    def gather_recv():
+        whole = GE.at[:, :, pl.ds(8, ry3)]
+        pltpu.make_async_copy(whole, whole, ga_recv.at[0]).wait()
+
+    def gather_sent():
         def one(d, carry):
-            pltpu.make_async_copy(packed, packed, ga_send.at[which, d]).wait()
+            pltpu.make_async_copy(PG, PG, ga_send.at[d]).wait()
             return carry
 
         lax.fori_loop(1, n, one, 0, unroll=True)
@@ -255,6 +290,8 @@
     start_all(source_halo)
     tell(0)
     start_all(beta1_halo)
+    beta2_window = window_copies(0, PB, GB)
+    start_all(beta2_window)
 
     def setup(level, Bl, CX, CY, CM, CP, Q, D, first, last, row, rows, hx, nx, ny):
         apart = 1 << level
@@ -333,41 +370,15 @@
     def down0(p, carry):
         i = H0 + 2 * p
         pair = residual(0, U0, S0, D0, coeffs0, i, HY, Y0) + residual(0, U0, S0, D0, coeffs0, i + 1, HY, Y0)
-        S1[H1 + p, pl.ds(HY, Y0 // 2)] = halve(pair, 1, p)
+        half = halve(pair, 1, p)
+        S1[H1 + p, pl.ds(HY, Y0 // 2)] = half
+        SZ1[H1 + p, pl.ds(HY, Y0 // 2)] = half
         return carry
 
     lax.fori_loop(0, X0 // 2, down0, 0, unroll=True)
     source1_halo = halo_copies(3, S1, X0 // 2, H1, Y0 // 2, 2, 2, 4)
     source1_late = late_copies(2, S1, LX1, LY1, X0 // 2, H1, Y0 // 2, 2, 4)
     start_all(source1_halo)
-    hear(1)
-    gather_start(0, PB, GB)
-    start_all(source1_late[0])
-    start_all(beta_late[0])
-    start_all(source_late[0])
-
-    recv_all(beta1_halo)
-    setup(1, B1, CX1, CY1, CM1, CP1, Q1, D1, 1, 17, row1, rows1, H1, X0 // 2, Y0 // 2)
-    recv_all(source1_halo)
-    first_sweep(V1, Q1, S1, 3, 15, row1, rows1)
-    sweep(1, V1, U1, S1, Q1, coeffs1, 4, 14, row1, rows1)
-    planes = []
-    for p in range(X0 // 4):
-        i = H1 + 2 * p
-        pair = residual(1, U1, S1, D1, coeffs1, i, HY, Y0 // 2) + residual(1, U1, S1, D1, coeffs1, i + 1, HY, Y0 // 2)
-        planes.append(halve(pair, 2, p))
-    PS[...] = pack(planes)
-    gather_start(1, PS, GS)
-
-    land_all(source1_late)
-    first_sweep(V1, Q1, S1, 1, 17, row1, rows1)
-    sweep(1, V1, U1, S1, Q1, coeffs1, 2, 16, row1, rows1)
-    land_all(beta_late)
-    land_all(source_late)
-    setup(0, B0, CX0, CY0, CM0, CP0, Q0, D0, 1, 23, row0, rows0, H0, X0, Y0)
-    first_sweep(V0, Q0, S0, 1, 23, row0, rows0)
-    sweep(0, V0, U0, S0, Q0, coeffs0, 2, 22, row0, rows0)
-
     def neighbours(v, level):
         st, zs = 1 << (level - 2), 1 << level
         before = [v[i - 1] for i in range(G)]
@@ -384,31 +395,31 @@
         zp = [roll(a, -zs, 1) for a in v]
         return xm, xp, ym, yp, zm, zp
 
-    def setup_whole(beta, C, level):
+    def setup_whole(beta, C, level, first, total_rows):
         st, zs = 1 << (level - 2), 1 << level
         h = 0.5 * 0.25**level
         near = neighbours(beta, level)
         shape = beta[0].shape
         lane = lane_of(shape)
-        row = lax.broadcasted_iota(jnp.int32, shape, 0)
+        row = lax.broadcasted_iota(jnp.int32, shape, 0) + first
+        inside = (row >= 0) & (row < total_rows)
         for i in range(G):
             ok = [
-                ((lane & 3) >= st) if i == 0 else None,
-                ((lane & 3) < 4 - st) if i == G - 1 else None,
-                row > 0,
-                row < shape[0] - 1,
-                lane >= zs,
-                lane < LANES - zs,
+                inside & ((lane & 3) >= st) if i == 0 else inside,
+                inside & ((lane & 3) < 4 - st) if i == G - 1 else inside,
+                (row > 0) & (row < total_rows),
+                (row >= 0) & (row < total_rows - 1),
+                inside & (lane >= zs),
+                inside & (lane < LANES - zs),
             ]
             total = 6.0 * beta[i]
             for d in range(6):
-                there = near[d][i] if ok[d] is None else jnp.where(ok[d], near[d][i], 0.0)
+                there = jnp.where(ok[d], near[d][i], 0.0)
                 total = total + there
-                face = h * (beta[i] + there)
-                C[d, i] = face if ok[d] is None else jnp.where(ok[d], face, 0.0)
+                C[d, i] = jnp.where(ok[d], h * (beta[i] + there), 0.0)
             diag = h * total
             C[6, i] = diag
-            C[7, i] = W / diag
+            C[7, i] = jnp.where(inside, W / diag, 0.0)
 
     def sum_across(v, C, level):
         near = neighbours(v, level)
@@ -443,22 +454,81 @@
             out.append(E[i, pl.ds(0, 2 * rows)])
         return out
 
-    gather_recv(0, GB)
-    beta2 = [GB[i] for i in range(G)]
-    setup_whole(beta2, C2, 2)
-    beta3 = coarsen(beta2, 2)
-    setup_whole(beta3, C3, 3)
+    recv_all(beta1_halo)
+    setup(1, B1, CX1, CY1, CM1, CP1, Q1, D1, 1, 17, row1, rows1, H1, X0 // 2, Y0 // 2)
+    first_sweep(V1, Q1, SZ1, H1, H1 + X0 // 2, HY, Y0 // 2)
+    sweep(1, V1, U1, SZ1, Q1, coeffs1, H1 - 1, H1 + X0 // 2 + 1, HY - 2, Y0 // 2 + 4)
+    planes = []
+    for p in range(-1, X0 // 4 + 1):
+        i = H1 + 2 * p
+        pair = residual(1, U1, SZ1, D1, coeffs1, i, HY - 2, Y0 // 2 + 4)
+        pair = pair + residual(1, U1, SZ1, D1, coeffs1, i + 1, HY - 2, Y0 // 2 + 4)
+        planes.append(halve(pair, 2, p + 1))
+    k = lane_of(planes[0].shape) & 3
+    Z2[g, pl.ds(7, 10)] = jnp.where(k == 3, planes[0], 0.0)
+    Z2[g + 1, pl.ds(7, 10)] = pack(planes[1:5])
+    Z2[g + 2, pl.ds(7, 10)] = jnp.where(k == 0, planes[5], 0.0)
+    recv_all(beta2_window)
+    setup_whole([GB[i] for i in range(G)], C2, 2, 8 * b - 8, ry2)
+    z2 = [Z2[i + 1] for i in range(G)]
+    v = [C2[7, i] * z2[i] for i in range(G)]
+    v = sweep_whole(v, z2, C2, 2)
+    total = sum_across(v, C2, 2)
+    for i in range(G):
+        E[i, pl.ds(0, 24)] = pair_lanes(pair_lanes(z2[i] - (C2[6, i] * v[i] - total[i]), 1), 4)
+        F[i + 1] = 0.125 * (E[i, pl.ds(4, 8, stride=2)] + E[i, pl.ds(5, 8, stride=2)])
+    slot = (lane_of((8, LANES)) & 1) + ((lane_of((8, LANES)) >> 1) & 2)
+    packed = jnp.where(slot == 2, F[g + 2], P3[...])
+    packed = jnp.where(slot == 1, F[g + 1], packed)
+    PG[...] = jnp.where(slot == 0, F[g], packed)
+    hear(1)
+    gather_start()
+    start_all(source1_late[0])
+    start_all(beta_late[0])
+    start_all(source_late[0])
+
+    recv_all(source1_halo)
+    first_sweep(V1, Q1, S1, 3, 15, row1, rows1)
+    sweep(1, V1, U1, S1, Q1, coeffs1, 4, 14, row1, rows1)
+    planes = []
+    for p in range(X0 // 4):
+        i = H1 + 2 * p
+        pair = residual(1, U1, S1, D1, coeffs1, i, HY, Y0 // 2) + residual(1, U1, S1, D1, coeffs1, i + 1, HY, Y0 // 2)
+        planes.append(halve(pair, 2, p))
+    PS[...] = pack(planes)
+    source2_window = window_copies(1, PS, GS)
+    start_all(source2_window)
+    GS[g, pl.ds(8, 8)] = PS[...]
+
+    land_all(source1_late)
+    first_sweep(V1, Q1, S1, 1, 17, row1, rows1)
+    sweep(1, V1, U1, S1, Q1, coeffs1, 2, 16, row1, rows1)
+    land_all(beta_late)
+    land_all(source_late)
+    setup(0, B0, CX0, CY0, CM0, CP0, Q0, D0, 1, 23, row0, rows0, H0, X0, Y0)
+    first_sweep(V0, Q0, S0, 1, 23, row0, rows0)
+    sweep(0, V0, U0, S0, Q0, coeffs0, 2, 22, row0, rows0)
+
+    gather_recv()
+    slot = (lane_of((ry3, LANES)) & 1) + ((lane_of((ry3, LANES)) >> 1) & 2)
+    parts = [GE[0, i, pl.ds(10, ry3)] + GE[1, i, pl.ds(6, ry3)] for i in range(G)]
+
+    def spread(v):
+        return pair_lanes(pair_lanes(v, 1), 4)
+
+    beta3 = [spread(jnp.where(slot == 3, a, 0.0)) for a in parts]
+    s3 = []
+    for i in range(G):
+        mine = jnp.where(slot == 1, parts[i], 0.0)
+        if i + 1 < G:
+            mine = jnp.where(slot == 0, parts[i + 1], mine)
+        if i > 0:
+            mine = jnp.where(slot == 2, parts[i - 1], mine)
+        s3.append(spread(mine))
+    setup_whole(beta3, C3, 3, 0, ry3)
     beta4 = coarsen(beta3, 3)
-    setup_whole(beta4, C4, 4)
-
-    gather_recv(1, GS)
-    s2 = [GS[i] for i in range(G)]
-    v = [C2[7, i] * s2[i] for i in range(G)]
-    v = sweep_whole(v, s2, C2, 2)
-    for i in range(G):
-        V2[i + 1, pl.ds(8, ry2)] = v[i]
-    total = sum_across(v, C2, 2)
-    s3 = coarsen([s2[i] - (C2[6, i] * v[i] - total[i]) for i in range(G)], 2)
+    setup_whole(beta4, C4, 4, 0, ry4)
+
     v = [C3[7, i] * s3[i] for i in range(G)]
     v = sweep_whole(v, s3, C3, 3)
     for i in range(G):
@@ -496,17 +566,22 @@
     v = [F3[0, i] + up[i] for i in range(G)]
     for _ in range(SWEEPS):
         v = sweep_whole(v, s3, C3, 3)
-    up = refine(v)
+    for i in range(G):
+        for odd in (0, 1):
+            E2[i, pl.ds(8 + odd, ry3, stride=2)] = v[i]
+    recv_all(source2_window)
     s2 = [GS[i] for i in range(G)]
-    v = [V2[i + 1, pl.ds(8, ry2)] + up[i] for i in range(G)]
+    v = [C2[7, i] * s2[i] for i in range(G)]
+    v = sweep_whole(v, s2, C2, 2)
+    v = [v[i] + E2[i, pl.ds(pl.multiple_of(b * 8, 8), 24)] for i in range(G)]
     for _ in range(SWEEPS):
         v = sweep_whole(v, s2, C2, 2)
     for i in range(G):
-        V2[i + 1, pl.ds(8, ry2)] = v[i]
+        V2[i + 1] = v[i]
 
     for x2 in range(-2, 6):
         k = x2 % 4
-        window = V2[g + 1 + x2 // 4, pl.ds(pl.multiple_of(b * 8, 8), 24)]
+        window = V2[g + 1 + x2 // 4]
         one = jnp.where((lane_of(window.shape) & 3) == k, window, 0.0)
         one = one + roll(one, 1 if k in (0, 2) else -1, 1)
         one = one + roll(one, 2 if k in (0, 1) else -2, 1)
@@ -540,8 +615,9 @@
     sent_all(beta_late[0])
     sent_all(source_late[0])
     sent_all(source1_late[0])
-    gather_sent(0, PB)
-    gather_sent(1, PS)
+    sent_all(beta2_window)
+    sent_all(source2_window)
+    gather_sent()
 
 
 def in_one_kernel(G, B, right_side, beta):
@@ -556,15 +632,22 @@
         + [level1] * 10
         + [
             pltpu.VMEM((8, Y0, LANES), F32),
+            level1,
             pltpu.VMEM((8, LANES), F32),
             pltpu.VMEM((8, LANES), F32),
-            pltpu.VMEM((G, 8 * B, LANES), F32),
-            pltpu.VMEM((G, 8 * B, LANES), F32),
-            pltpu.VMEM((G + 2, 8 * B + 16, LANES), F32),
-            pltpu.VMEM((8, G, 8 * B, LANES), F32),
+            pltpu.VMEM((8, LANES), F32),
+            pltpu.VMEM((8, LANES), F32),
+            pltpu.VMEM((G, 24, LANES), F32),
+            pltpu.VMEM((G, 24, LANES), F32),
+            pltpu.VMEM((2, G, 4 * B + 16, LANES), F32),
+            pltpu.VMEM((G + 2, 24, LANES), F32),
+            pltpu.VMEM((G + 2, 24, LANES), F32),
+            pltpu.VMEM((8, G, 24, LANES), F32),
             pltpu.VMEM((8, G, 4 * B, LANES), F32),
             pltpu.VMEM((8, G, 2 * B, LANES), F32),
             pltpu.VMEM((G, 8 * B, LANES), F32),
+            pltpu.VMEM((G, 8 * B + 16, LANES), F32),
+            pltpu.VMEM((G + 2, 8, LANES), F32),
             pltpu.VMEM((2, G, 4 * B, LANES), F32),
             pltpu.VMEM((2, 2, 1, Y0, LANES), F32),
             pltpu.VMEM((2, 2, X0, 8, LANES), F32),
@@ -574,9 +657,11 @@
             pltpu.SemaphoreType.DMA((4, 8)),
             pltpu.SemaphoreType.DMA((3, 4)),
             pltpu.SemaphoreType.DMA((3, 4)),
-            pltpu.SemaphoreType.DMA((2, G * B)),
-            pltpu.SemaphoreType.DMA((2,)),
-            pltpu.SemaphoreType.REGULAR((8,)),
+            pltpu.SemaphoreType.DMA((2, 3 * G)),
+            pltpu.SemaphoreType.DMA((2, 3 * G)),
+            pltpu.SemaphoreType.DMA((G * B,)),
+            pltpu.SemaphoreType.DMA((1,)),
+            pltpu.SemaphoreType.REGULAR((2,)),
             pltpu.SemaphoreType.DMA((2,)),
         ],
         compiler_params=pltpu.CompilerParams(

time: 28.5 us -> 25.7 us (0.902)
  Pallas kernels: 27.6 us -> 24.8 us
    pallas_call x1, Pallas kernels: 27.6 us -> 24.8 us  [in_one_kernel(): pl.pallas_call(functools.partial(kernel, G, B), out_shape=jax.ShapeDtypeS...]
where the time goes in v2:
time: 25.7 us; the launch traced here: 25.5 us
  Pallas kernels  24.8 us (96%)
  local copies, waits for them, and re-layouts  0.71 us (3%)
    pallas_call x1, Pallas kernels, in_one_kernel(): pl.pallas_call(functools.partial(kernel, G, B), out_shape=jax.ShapeDtypeS...  24.8 us
    unnamed x1, local copies, waits for them, and re-layouts  0.71 us

profile of v2, /device:TPU:0, one launch (start us, length us, event | category | flops | bytes accessed | tf_op | source)
XLA Modules:
  0.0 25.5 jit_solution(16875216778720527499)
XLA Ops:
  0.0 24.8 %shard_map.28 = f32[16,32,128]{2,1,0:T(8,128)S(1)} custom-call(f32[16,32,128]{2,1,0:T(8,128)} %rs_ref.1, f32[16,32,128]{2,1,0:T(8,128)} %be_ref.1), custom_call_target="tpu_custom_call" | custom-call | tf_op jit(solution)/shard_map/pallas_call | solution.py:626
  24.8 0.7 %copy.4 = f32[16,32,128]{2,1,0:T(8,128)} copy(f32[16,32,128]{2,1,0:T(8,128)S(1)} %shard_map.28) | data formatting | bytes 524288

commit v3 on v2

--- a/solution.py
+++ b/solution.py
@@ -46,7 +46,7 @@
     G, B, rs_ref, be_ref, out_ref,
     B0, S0, V0, U0, CX0, CY0, CM0, CP0, Q0, D0,
     B1, S1, V1, U1, CX1, CY1, CM1, CP1, Q1, D1,
-    T, SZ1, PB, PS, P3, PG, GB, GS, GE, V2, Z2, C2, C3, C4, E, E2, F, F3, LX0, LY0, LX1, LY1,
+    T, SZ0, SZ1, PB, PS, P3, PG, GB, GS, GL, GE, V2, Z2, C2, C3, C4, E, E2, F, F3, LX0, LY0, LX1, LY1,
     halo_send, halo_recv, late_send, late_recv, win_send, win_recv, ga_send, ga_recv, rounds, loc_sem,
 ):
     n = G * B
@@ -60,6 +60,8 @@
     load_s = pltpu.make_async_copy(rs_ref, S0.at[own0[0], own0[1]], loc_sem.at[1])
     load_b.start()
     load_s.start()
+    load_z = pltpu.make_async_copy(rs_ref, SZ0.at[own0[0], own0[1]], loc_sem.at[2])
+    load_z.start()
 
     barrier = pltpu.get_barrier_semaphore()
 
@@ -124,22 +126,6 @@
         @pl.when(b == B - 1)
         def _():
             ref[:, pl.ds(HY + ny, HY)] = jnp.zeros((planes, HY, LANES), F32)
-
-    for ref in (SZ1, V1, U1, V2, Z2):
-        ref[...] = jnp.zeros(ref.shape, F32)
-    for side, edge in ((0, 0), (16, B - 1)):
-        for ref in (GB, GS):
-
-            @pl.when(b == edge)
-            def _():
-                ref[:, pl.ds(side, 8)] = jnp.zeros((G, 8, LANES), F32)
-
-    E2[:, pl.ds(0, 8)] = jnp.zeros((G, 8, LANES), F32)
-    E2[:, pl.ds(8 + ry2, 8)] = jnp.zeros((G, 8, LANES), F32)
-    F[0] = jnp.zeros((8, LANES), F32)
-    F[G + 1] = jnp.zeros((8, LANES), F32)
-    GE[:, :, pl.ds(0, 8)] = jnp.zeros((2, G, 8, LANES), F32)
-    GE[:, :, pl.ds(8 + ry3, 8)] = jnp.zeros((2, G, 8, LANES), F32)
 
     load_b.wait()
 
@@ -169,6 +155,7 @@
     P3[pl.ds(2, 4)] = 0.125 * (T[0, pl.ds(0, 4, stride=2)] + T[0, pl.ds(1, 4, stride=2)])
 
     load_s.wait()
+    load_z.wait()
     pl.semaphore_wait(barrier, expected)
 
     def there_from(dx, dy):
@@ -234,7 +221,7 @@
         for copy, there, _ in copies:
             pl.when(there)(copy.wait_send)
 
-    def window_copies(kind, packed, whole):
+    def window_copies(kind, packed, spot):
         made = []
         for o in range(G):
             for dy in (-1, 0, 1):
@@ -242,8 +229,8 @@
                     continue
                 at = 3 * o + dy + 1
                 copy = pltpu.make_async_remote_copy(
-                    src_ref=packed,
-                    dst_ref=whole.at[g, pl.ds(8 - 8 * dy, 8)],
+                    src_ref=packed(dy),
+                    dst_ref=spot(dy),
                     send_sem=win_send.at[kind, at],
                     recv_sem=win_recv.at[kind, at],
                     device_id=((g + o) % G, b + dy),
@@ -261,7 +248,7 @@
             pltpu.make_async_remote_copy(
                 src_ref=PG,
                 dst_ref=spot,
-                send_sem=ga_send.at[d],
+                send_sem=ga_send.at[0],
                 recv_sem=ga_recv.at[0],
                 device_id=(peer // B, peer % B),
                 device_id_type=MESH,
@@ -275,23 +262,47 @@
         pltpu.make_async_copy(whole, whole, ga_recv.at[0]).wait()
 
     def gather_sent():
-        def one(d, carry):
-            pltpu.make_async_copy(PG, PG, ga_send.at[d]).wait()
-            return carry
-
-        lax.fori_loop(1, n, one, 0, unroll=True)
-
-    beta_halo = halo_copies(0, B0, X0, H0, Y0, 3, 3, 3)
-    source_halo = halo_copies(1, S0, X0, H0, Y0, 2, 2, 2)
-    beta1_halo = halo_copies(2, B1, X0 // 2, H1, Y0 // 2, 5, 5, 5)
-    beta_late = late_copies(0, B0, LX0.at[0], LY0.at[0], X0, H0, Y0, 3, 4)
-    source_late = late_copies(1, S0, LX0.at[1], LY0.at[1], X0, H0, Y0, 2, 3)
+        room = CX0.at[pl.ds(0, 8), pl.ds(0, n - 1)]
+        pltpu.make_async_copy(room, room, ga_send.at[0]).wait()
+
+    beta_halo = halo_copies(0, B0, X0, H0, Y0, 2, 2, 3)
+    source_halo = halo_copies(1, S0, X0, H0, Y0, 3, 3, 2)
+    beta1_halo = halo_copies(2, B1, X0 // 2, H1, Y0 // 2, 3, 3, 5)
+    beta2_window = window_copies(0, lambda dy: PB, lambda dy: GB.at[g, pl.ds(8 - 8 * dy, 8)])
+    beta_late = late_copies(0, B0, LX0, LY0, X0, H0, Y0, 2, 4)
+    beta1_late = late_copies(1, B1, LX1, LY1, X0 // 2, H1, Y0 // 2, 3, 5)
     start_all(beta_halo)
-    start_all(source_halo)
+
+    for ref in (SZ1, V1, U1, V2, Z2, GS):
+        ref[...] = jnp.zeros(ref.shape, F32)
+    for ref, deep in ((SZ0, 2), (V0, 2), (U0, 3)):
+        for x in (H0 - deep, H0 + X0 + deep - 2):
+            ref[pl.ds(x, 2)] = jnp.zeros((2, Y0 + 2 * HY, LANES), F32)
+        for y in (0, HY + Y0):
+            ref[pl.ds(H0 - 1, X0 + 2), pl.ds(y, HY)] = jnp.zeros((X0 + 2, HY, LANES), F32)
+    for ref, nx, hx, ny, near in ((B0, X0, H0, Y0, 2), (B1, X0 // 2, H1, Y0 // 2, 3)):
+        for x in (hx - near - 2, hx + nx + near):
+            ref[pl.ds(x, 2), pl.ds(HY, ny)] = jnp.zeros((2, ny, LANES), F32)
+        for y in (HY - near - 2, HY + ny + near):
+            ref[pl.ds(hx, nx), pl.ds(y, 2)] = jnp.zeros((nx, 2, LANES), F32)
+    CY1[:, pl.ds(HY + Y0 // 2 + 4, 4)] = jnp.zeros((X0 // 2 + 2 * H1, 4, LANES), F32)
+    for side, edge in ((0, 0), (2, B - 1)):
+
+        @pl.when(b == edge)
+        def _():
+            GB[:, pl.ds(8 * side, 8)] = jnp.zeros((G, 8, LANES), F32)
+            GL[:, side] = jnp.zeros((G, 2, 16, LANES), F32)
+
+    E2[:, pl.ds(0, 8)] = jnp.zeros((G, 8, LANES), F32)
+    E2[:, pl.ds(8 + ry2, 8)] = jnp.zeros((G, 8, LANES), F32)
+    F[0] = jnp.zeros((8, LANES), F32)
+    F[G + 1] = jnp.zeros((8, LANES), F32)
+    GE[:, :, pl.ds(0, 8)] = jnp.zeros((2, G, 8, LANES), F32)
+    GE[:, :, pl.ds(8 + ry3, 8)] = jnp.zeros((2, G, 8, LANES), F32)
+
+    start_all(beta1_halo)
+    start_all(beta2_window)
     tell(0)
-    start_all(beta1_halo)
-    beta2_window = window_copies(0, PB, GB)
-    start_all(beta2_window)
 
     def setup(level, Bl, CX, CY, CM, CP, Q, D, first, last, row, rows, hx, nx, ny):
         apart = 1 << level
@@ -362,23 +373,9 @@
     recv_all(beta_halo)
     hear(0)
     tell(1)
-    setup(0, B0, CX0, CY0, CM0, CP0, Q0, D0, 2, 22, row0, rows0, H0, X0, Y0)
-    recv_all(source_halo)
-    first_sweep(V0, Q0, S0, 2, 22, row0, rows0)
-    sweep(0, V0, U0, S0, Q0, coeffs0, 3, 21, row0, rows0)
-
-    def down0(p, carry):
-        i = H0 + 2 * p
-        pair = residual(0, U0, S0, D0, coeffs0, i, HY, Y0) + residual(0, U0, S0, D0, coeffs0, i + 1, HY, Y0)
-        half = halve(pair, 1, p)
-        S1[H1 + p, pl.ds(HY, Y0 // 2)] = half
-        SZ1[H1 + p, pl.ds(HY, Y0 // 2)] = half
-        return carry
-
-    lax.fori_loop(0, X0 // 2, down0, 0, unroll=True)
-    source1_halo = halo_copies(3, S1, X0 // 2, H1, Y0 // 2, 2, 2, 4)
-    source1_late = late_copies(2, S1, LX1, LY1, X0 // 2, H1, Y0 // 2, 2, 4)
-    start_all(source1_halo)
+    start_all(source_halo)
+    start_all(beta_late[0])
+    start_all(beta1_late[0])
     def neighbours(v, level):
         st, zs = 1 << (level - 2), 1 << level
         before = [v[i - 1] for i in range(G)]
@@ -454,20 +451,37 @@
             out.append(E[i, pl.ds(0, 2 * rows)])
         return out
 
+    def pair_of(level, V, S, D, coeffs, first, second, row, rows):
+        one = [residual(level, V, S, D, coeffs, i, row, rows) for i in (first, second) if i is not None]
+        return one[0] if len(one) == 1 else one[0] + one[1]
+
+    setup(0, B0, CX0, CY0, CM0, CP0, Q0, D0, 2, 23, row0, rows0, H0, X0, Y0)
+    first_sweep(V0, Q0, SZ0, H0, H0 + X0, HY, Y0)
+    sweep(0, V0, U0, SZ0, Q0, coeffs0, H0 - 1, H0 + X0 + 1, HY - 2, Y0 + 4)
+    for p in range(-1, X0 // 2 + 1):
+        i = H0 + 2 * p
+        SZ1[H1 + p, pl.ds(HY - 1, Y0 // 2 + 2)] = halve(
+            pair_of(0, U0, SZ0, D0, coeffs0, i, i + 1, HY - 2, Y0 + 4), 1, p + 1
+        )
     recv_all(beta1_halo)
     setup(1, B1, CX1, CY1, CM1, CP1, Q1, D1, 1, 17, row1, rows1, H1, X0 // 2, Y0 // 2)
-    first_sweep(V1, Q1, SZ1, H1, H1 + X0 // 2, HY, Y0 // 2)
-    sweep(1, V1, U1, SZ1, Q1, coeffs1, H1 - 1, H1 + X0 // 2 + 1, HY - 2, Y0 // 2 + 4)
+    first_sweep(V1, Q1, SZ1, H1 - 1, H1 + X0 // 2 + 1, HY - 1, Y0 // 2 + 2)
+    sweep(1, V1, U1, SZ1, Q1, coeffs1, H1 - 2, H1 + X0 // 2 + 2, HY - 2, Y0 // 2 + 4)
+    last = X0 // 4 + 1
     planes = []
-    for p in range(-1, X0 // 4 + 1):
+    for p in range(-2, last + 1):
         i = H1 + 2 * p
-        pair = residual(1, U1, SZ1, D1, coeffs1, i, HY - 2, Y0 // 2 + 4)
-        pair = pair + residual(1, U1, SZ1, D1, coeffs1, i + 1, HY - 2, Y0 // 2 + 4)
-        planes.append(halve(pair, 2, p + 1))
+        pair = pair_of(
+            1, U1, SZ1, D1, coeffs1, None if p == -2 else i, None if p == last else i + 1, HY - 4, Y0 // 2 + 8
+        )
+        planes.append(halve(pair, 2, p + 2))
     k = lane_of(planes[0].shape) & 3
-    Z2[g, pl.ds(7, 10)] = jnp.where(k == 3, planes[0], 0.0)
-    Z2[g + 1, pl.ds(7, 10)] = pack(planes[1:5])
-    Z2[g + 2, pl.ds(7, 10)] = jnp.where(k == 0, planes[5], 0.0)
+    middle, sides = pack(planes[2:6]), pack(planes[6:8] + planes[0:2])
+    PS[0, pl.ds(0, 12)] = middle
+    PS[1, pl.ds(0, 12)] = sides
+    Z2[g, pl.ds(6, 12)] = jnp.where(k >= 2, sides, 0.0)
+    Z2[g + 1, pl.ds(6, 12)] = middle
+    Z2[g + 2, pl.ds(6, 12)] = jnp.where(k < 2, sides, 0.0)
     recv_all(beta2_window)
     setup_whole([GB[i] for i in range(G)], C2, 2, 8 * b - 8, ry2)
     z2 = [Z2[i + 1] for i in range(G)]
@@ -483,32 +497,29 @@
     PG[...] = jnp.where(slot == 0, F[g], packed)
     hear(1)
     gather_start()
-    start_all(source1_late[0])
-    start_all(beta_late[0])
-    start_all(source_late[0])
-
-    recv_all(source1_halo)
-    first_sweep(V1, Q1, S1, 3, 15, row1, rows1)
-    sweep(1, V1, U1, S1, Q1, coeffs1, 4, 14, row1, rows1)
-    planes = []
-    for p in range(X0 // 4):
-        i = H1 + 2 * p
-        pair = residual(1, U1, S1, D1, coeffs1, i, HY, Y0 // 2) + residual(1, U1, S1, D1, coeffs1, i + 1, HY, Y0 // 2)
-        planes.append(halve(pair, 2, p))
-    PS[...] = pack(planes)
-    source2_window = window_copies(1, PS, GS)
+    recv_all(source_halo)
+    part = {-1: pl.ds(0, 8), 0: pl.ds(0, 12), 1: pl.ds(4, 8)}
+    source2_window = window_copies(1, lambda dy: PS.at[:, part[dy]], lambda dy: GL.at[g, 1 - dy, :, part[dy]])
     start_all(source2_window)
-    GS[g, pl.ds(8, 8)] = PS[...]
-
-    land_all(source1_late)
-    first_sweep(V1, Q1, S1, 1, 17, row1, rows1)
-    sweep(1, V1, U1, S1, Q1, coeffs1, 2, 16, row1, rows1)
+    GL[g, 1] = PS[...]
+
     land_all(beta_late)
-    land_all(source_late)
     setup(0, B0, CX0, CY0, CM0, CP0, Q0, D0, 1, 23, row0, rows0, H0, X0, Y0)
     first_sweep(V0, Q0, S0, 1, 23, row0, rows0)
     sweep(0, V0, U0, S0, Q0, coeffs0, 2, 22, row0, rows0)
-
+    for p in range(X0 // 2):
+        i = H0 + 2 * p
+        S1[H1 + p, pl.ds(HY, Y0 // 2)] = halve(pair_of(0, U0, S0, D0, coeffs0, i, i + 1, HY, Y0), 1, p)
+    source1_halo = halo_copies(3, S1, X0 // 2, H1, Y0 // 2, 4, 4, 4)
+    start_all(source1_halo)
+    land_all(beta1_late)
+    setup(1, B1, CX1, CY1, CM1, CP1, Q1, D1, 1, 17, row1, rows1, H1, X0 // 2, Y0 // 2)
+
+    for copies in (beta_halo, beta1_halo, beta2_window, source_halo, beta_late[0], beta1_late[0]):
+        sent_all(copies)
+    recv_all(source1_halo)
+    first_sweep(V1, Q1, S1, 1, 17, row1, rows1)
+    sweep(1, V1, U1, S1, Q1, coeffs1, 2, 16, row1, rows1)
     gather_recv()
     slot = (lane_of((ry3, LANES)) & 1) + ((lane_of((ry3, LANES)) >> 1) & 2)
     parts = [GE[0, i, pl.ds(10, ry3)] + GE[1, i, pl.ds(6, ry3)] for i in range(G)]
@@ -546,20 +557,24 @@
             part = part + acc[j : j + 8]
         return jnp.sum(jnp.sum(part, axis=0, keepdims=True), axis=1, keepdims=True)
 
-    def cg(step, carry):
-        x, r, p, rr = carry
-        near = sum_across(p, C4, 4)
-        q = [C4[6, i] * p[i] - near[i] for i in range(G)]
-        alpha = rr / dot(p, q)
-        x = [x[i] + alpha * p[i] for i in range(G)]
+    def apply(r):
+        near = sum_across(r, C4, 4)
+        return [C4[6, i] * r[i] - near[i] for i in range(G)]
+
+    p, r, q = s4, s4, apply(s4)
+    rr = dot(r, r)
+    alpha = rr / dot(r, q)
+    x4 = [alpha * p[i] for i in range(G)]
+    for _ in range(COARSE - 1):
         r = [r[i] - alpha * q[i] for i in range(G)]
-        new = dot(r, r)
+        w = apply(r)
+        new, delta = dot(r, r), dot(r, w)
         ratio = new / rr
+        alpha = new / (delta - ratio * (new / alpha))
         p = [r[i] + ratio * p[i] for i in range(G)]
-        return x, r, p, new
-
-    zero = [jnp.zeros((ry4, LANES), F32) for i in range(G)]
-    x4 = lax.fori_loop(0, COARSE, cg, (zero, s4, s4, dot(s4, s4)), unroll=True)[0]
+        q = [w[i] + ratio * q[i] for i in range(G)]
+        x4 = [x4[i] + alpha * p[i] for i in range(G)]
+        rr = new
 
     up = refine(x4)
     s3 = [F3[1, i] for i in range(G)]
@@ -570,7 +585,17 @@
         for odd in (0, 1):
             E2[i, pl.ds(8 + odd, ry3, stride=2)] = v[i]
     recv_all(source2_window)
-    s2 = [GS[i] for i in range(G)]
+    for j in (0, 1):
+        for i in range(G):
+            GS[j, i, pl.ds(10, 8)] = GL[i, 0, j, pl.ds(4, 8)]
+            GS[j, i, pl.ds(22, 8)] = GL[i, 2, j, pl.ds(0, 8)]
+            GS[j, i, pl.ds(14, 12)] = GS[j, i, pl.ds(14, 12)] + GL[i, 1, j, pl.ds(0, 12)]
+    k = lane_of((24, LANES)) & 3
+    s2 = []
+    for i in range(G):
+        left = GS[1, i - 1, pl.ds(8, 24)] if i > 0 else 0.0
+        right = GS[1, i + 1, pl.ds(8, 24)] if i + 1 < G else 0.0
+        s2.append(GS[0, i, pl.ds(8, 24)] + jnp.where(k < 2, left, right))
     v = [C2[7, i] * s2[i] for i in range(G)]
     v = sweep_whole(v, s2, C2, 2)
     v = [v[i] + E2[i, pl.ds(pl.multiple_of(b * 8, 8), 24)] for i in range(G)]
@@ -608,14 +633,7 @@
     sweep(0, U0, V0, S0, Q0, coeffs0, 3, 21, row0, rows0)
     sweep(0, V0, out_ref, S0, Q0, coeffs0, 4, 20, HY, Y0, H0, HY)
 
-    sent_all(beta_halo)
-    sent_all(source_halo)
-    sent_all(beta1_halo)
     sent_all(source1_halo)
-    sent_all(beta_late[0])
-    sent_all(source_late[0])
-    sent_all(source1_late[0])
-    sent_all(beta2_window)
     sent_all(source2_window)
     gather_sent()
 
@@ -631,14 +649,16 @@
         scratch_shapes=[level0] * 10
         + [level1] * 10
         + [
-            pltpu.VMEM((8, Y0, LANES), F32),
+            pltpu.VMEM((12, Y0 + 8, LANES), F32),
+            level0,
             level1,
             pltpu.VMEM((8, LANES), F32),
-            pltpu.VMEM((8, LANES), F32),
+            pltpu.VMEM((2, 16, LANES), F32),
             pltpu.VMEM((8, LANES), F32),
             pltpu.VMEM((8, LANES), F32),
             pltpu.VMEM((G, 24, LANES), F32),
-            pltpu.VMEM((G, 24, LANES), F32),
+            pltpu.VMEM((2, G, 40, LANES), F32),
+            pltpu.VMEM((G, 3, 2, 16, LANES), F32),
             pltpu.VMEM((2, G, 4 * B + 16, LANES), F32),
             pltpu.VMEM((G + 2, 24, LANES), F32),
             pltpu.VMEM((G + 2, 24, LANES), F32),
@@ -649,20 +669,20 @@
             pltpu.VMEM((G, 8 * B + 16, LANES), F32),
             pltpu.VMEM((G + 2, 8, LANES), F32),
             pltpu.VMEM((2, G, 4 * B, LANES), F32),
-            pltpu.VMEM((2, 2, 1, Y0, LANES), F32),
-            pltpu.VMEM((2, 2, X0, 8, LANES), F32),
+            pltpu.VMEM((2, 2, Y0, LANES), F32),
+            pltpu.VMEM((2, X0, 8, LANES), F32),
             pltpu.VMEM((2, 2, Y0 // 2, LANES), F32),
             pltpu.VMEM((2, X0 // 2, 8, LANES), F32),
             pltpu.SemaphoreType.DMA((4, 8)),
             pltpu.SemaphoreType.DMA((4, 8)),
-            pltpu.SemaphoreType.DMA((3, 4)),
-            pltpu.SemaphoreType.DMA((3, 4)),
+            pltpu.SemaphoreType.DMA((2, 4)),
+            pltpu.SemaphoreType.DMA((2, 4)),
             pltpu.SemaphoreType.DMA((2, 3 * G)),
             pltpu.SemaphoreType.DMA((2, 3 * G)),
-            pltpu.SemaphoreType.DMA((G * B,)),
+            pltpu.SemaphoreType.DMA((1,)),
             pltpu.SemaphoreType.DMA((1,)),
             pltpu.SemaphoreType.REGULAR((2,)),
-            pltpu.SemaphoreType.DMA((2,)),
+            pltpu.SemaphoreType.DMA((3,)),
         ],
         compiler_params=pltpu.CompilerParams(
             collective_id=0, has_side_effects=True, vmem_limit_bytes=40 * 1024 * 1024

time: 25.7 us -> 23.4 us (0.911)
  Pallas kernels: 24.8 us -> 22.5 us
    pallas_call x1, Pallas kernels: 24.8 us -> 22.5 us  [in_one_kernel(): pl.pallas_call(functools.partial(kernel, G, B), out_shape=jax.ShapeDtypeS...]
where the time goes in v3:
time: 23.4 us; the launch traced here: 23.2 us
  Pallas kernels  22.5 us (96%)
  local copies, waits for them, and re-layouts  0.71 us (3%)
    pallas_call x1, Pallas kernels, in_one_kernel(): pl.pallas_call(functools.partial(kernel, G, B), out_shape=jax.ShapeDtypeS...  22.5 us
    unnamed x1, local copies, waits for them, and re-layouts  0.71 us

profile of v3, /device:TPU:0, one launch (start us, length us, event | category | flops | bytes accessed | tf_op | source)
XLA Modules:
  0.0 23.2 jit_solution(4849875620668999625)
XLA Ops:
  0.0 22.5 %shard_map.28 = f32[16,32,128]{2,1,0:T(8,128)S(1)} custom-call(f32[16,32,128]{2,1,0:T(8,128)} %rs_ref.1, f32[16,32,128]{2,1,0:T(8,128)} %be_ref.1), custom_call_target="tpu_custom_call" | custom-call | tf_op jit(solution)/shard_map/pallas_call | solution.py:644
  22.5 0.7 %copy.4 = f32[16,32,128]{2,1,0:T(8,128)} copy(f32[16,32,128]{2,1,0:T(8,128)S(1)} %shard_map.28) | data formatting | bytes 524288

commit v4 on v3

--- a/solution.py
+++ b/solution.py
@@ -44,8 +44,8 @@
 
 def kernel(
     G, B, rs_ref, be_ref, out_ref,
-    B0, S0, V0, U0, CX0, CY0, CM0, CP0, Q0, D0,
-    B1, S1, V1, U1, CX1, CY1, CM1, CP1, Q1, D1,
+    B0, S0, V0, U0, CX0, CY0, CM0, CP0, Q0,
+    B1, S1, V1, U1, CX1, CY1, CM1, CP1, Q1,
     T, SZ0, SZ1, PB, PS, P3, PG, GB, GS, GL, GE, V2, Z2, C2, C3, C4, E, E2, F, F3, LX0, LY0, LX1, LY1,
     halo_send, halo_recv, late_send, late_recv, win_send, win_recv, ga_send, ga_recv, rounds, loc_sem,
 ):
@@ -285,6 +285,7 @@
             ref[pl.ds(x, 2), pl.ds(HY, ny)] = jnp.zeros((2, ny, LANES), F32)
         for y in (HY - near - 2, HY + ny + near):
             ref[pl.ds(hx, nx), pl.ds(y, 2)] = jnp.zeros((nx, 2, LANES), F32)
+    CX1[X0 // 2 + 2 * H1 - 1] = jnp.zeros((Y0 // 2 + 2 * HY, LANES), F32)
     CY1[:, pl.ds(HY + Y0 // 2 + 4, 4)] = jnp.zeros((X0 // 2 + 2 * H1, 4, LANES), F32)
     for side, edge in ((0, 0), (2, B - 1)):
 
@@ -304,7 +305,7 @@
     start_all(beta2_window)
     tell(0)
 
-    def setup(level, Bl, CX, CY, CM, CP, Q, D, first, last, row, rows, hx, nx, ny):
+    def setup(level, Bl, CX, CY, CM, CP, Q, first, last, row, rows, hx, nx, ny):
         apart = 1 << level
         h = 0.5 * 0.25**level
 
@@ -325,7 +326,6 @@
             CM[i, at] = jnp.where(low, h * (c + zm), 0.0)
             CP[i, at] = jnp.where(high, h * (c + zp), 0.0)
             d = h * (6.0 * c + ((xm + xp) + (ym + yp) + (zm + zp)))
-            D[i, at] = d
             x = g * nx + i - hx
             y = lax.broadcasted_iota(jnp.int32, c.shape, 0) + (b * ny + row - HY)
             inside = (y >= 0) & (y < B * ny) & (x >= 0) & (x < G * nx)
@@ -360,10 +360,6 @@
             return carry
 
         lax.fori_loop(first, last, plane, 0, unroll=True)
-
-    def residual(level, V, S, D, coeffs, i, row, rows):
-        v, total = across(level, V, *coeffs, i, row, rows)
-        return S[i, pl.ds(row, rows)] - (D[i, pl.ds(row, rows)] * v - total)
 
     coeffs0 = (CX0, CY0, CM0, CP0)
     coeffs1 = (CX1, CY1, CM1, CP1)
@@ -451,30 +447,50 @@
             out.append(E[i, pl.ds(0, 2 * rows)])
         return out
 
-    def pair_of(level, V, S, D, coeffs, first, second, row, rows):
-        one = [residual(level, V, S, D, coeffs, i, row, rows) for i in (first, second) if i is not None]
-        return one[0] if len(one) == 1 else one[0] + one[1]
-
-    setup(0, B0, CX0, CY0, CM0, CP0, Q0, D0, 2, 23, row0, rows0, H0, X0, Y0)
+    def fluxes(level, V, S, Bl, coeffs, i, row, rows, slot):
+        CX, CY, CM, _ = coeffs
+        apart = 1 << level
+        at, more, less = pl.ds(row, rows), pl.ds(row, rows + 1), pl.ds(row - 1, rows + 1)
+        v, w = V[i, at], V[i + 1, at]
+        lane = lane_of(v.shape)
+        edge = (lane < apart) | (lane >= LANES - apart)
+        wall = jnp.where(edge, (0.5 * 0.25**level) * (Bl[i, at] * v + Bl[i + 1, at] * w), 0.0)
+        T[slot, pl.ds(0, rows)] = (S[i, at] + S[i + 1, at]) - (
+            CX[i, at] * (v - V[i - 1, at]) + CX[i + 2, at] * (w - V[i + 2, at]) + wall
+        )
+        T[slot + 12, pl.ds(0, rows + 1)] = CY[i, more] * (V[i, more] - V[i, less]) + CY[i + 1, more] * (
+            V[i + 1, more] - V[i + 1, less]
+        )
+        T[slot + 24, pl.ds(0, rows)] = CM[i, at] * (v - roll(v, apart, 1)) + CM[i + 1, at] * (w - roll(w, apart, 1))
+
+    def restricted(level, half, slot):
+        apart = 1 << level
+
+        def every(k, first):
+            return T[k, pl.ds(first, half, stride=2)]
+
+        total = (every(slot, 0) + every(slot, 1)) - (every(slot + 12, 0) - every(slot + 12, 2))
+        z = every(slot + 24, 0) + every(slot + 24, 1)
+        z = jnp.where((lane_of(z.shape) & apart) == 0, z - roll(z, -2 * apart, 1), 0.0)
+        return 0.125 * pair_lanes(total - z, apart)
+
+    setup(0, B0, CX0, CY0, CM0, CP0, Q0, 2, 23, row0, rows0, H0, X0, Y0)
     first_sweep(V0, Q0, SZ0, H0, H0 + X0, HY, Y0)
     sweep(0, V0, U0, SZ0, Q0, coeffs0, H0 - 1, H0 + X0 + 1, HY - 2, Y0 + 4)
     for p in range(-1, X0 // 2 + 1):
-        i = H0 + 2 * p
-        SZ1[H1 + p, pl.ds(HY - 1, Y0 // 2 + 2)] = halve(
-            pair_of(0, U0, SZ0, D0, coeffs0, i, i + 1, HY - 2, Y0 + 4), 1, p + 1
-        )
+        fluxes(0, U0, SZ0, B0, coeffs0, H0 + 2 * p, HY - 2, Y0 + 4, p + 1)
+    for p in range(-1, X0 // 2 + 1):
+        SZ1[H1 + p, pl.ds(HY - 1, Y0 // 2 + 2)] = restricted(0, Y0 // 2 + 2, p + 1)
     recv_all(beta1_halo)
-    setup(1, B1, CX1, CY1, CM1, CP1, Q1, D1, 1, 17, row1, rows1, H1, X0 // 2, Y0 // 2)
+    setup(1, B1, CX1, CY1, CM1, CP1, Q1, 1, 17, row1, rows1, H1, X0 // 2, Y0 // 2)
     first_sweep(V1, Q1, SZ1, H1 - 1, H1 + X0 // 2 + 1, HY - 1, Y0 // 2 + 2)
     sweep(1, V1, U1, SZ1, Q1, coeffs1, H1 - 2, H1 + X0 // 2 + 2, HY - 2, Y0 // 2 + 4)
     last = X0 // 4 + 1
     planes = []
     for p in range(-2, last + 1):
-        i = H1 + 2 * p
-        pair = pair_of(
-            1, U1, SZ1, D1, coeffs1, None if p == -2 else i, None if p == last else i + 1, HY - 4, Y0 // 2 + 8
-        )
-        planes.append(halve(pair, 2, p + 2))
+        fluxes(1, U1, SZ1, B1, coeffs1, H1 + 2 * p, HY - 4, Y0 // 2 + 8, p + 2)
+    for p in range(-2, last + 1):
+        planes.append(restricted(1, Y0 // 4 + 4, p + 2))
     k = lane_of(planes[0].shape) & 3
     middle, sides = pack(planes[2:6]), pack(planes[6:8] + planes[0:2])
     PS[0, pl.ds(0, 12)] = middle
@@ -504,16 +520,17 @@
     GL[g, 1] = PS[...]
 
     land_all(beta_late)
-    setup(0, B0, CX0, CY0, CM0, CP0, Q0, D0, 1, 23, row0, rows0, H0, X0, Y0)
+    setup(0, B0, CX0, CY0, CM0, CP0, Q0, 1, 23, row0, rows0, H0, X0, Y0)
     first_sweep(V0, Q0, S0, 1, 23, row0, rows0)
     sweep(0, V0, U0, S0, Q0, coeffs0, 2, 22, row0, rows0)
     for p in range(X0 // 2):
-        i = H0 + 2 * p
-        S1[H1 + p, pl.ds(HY, Y0 // 2)] = halve(pair_of(0, U0, S0, D0, coeffs0, i, i + 1, HY, Y0), 1, p)
+        fluxes(0, U0, S0, B0, coeffs0, H0 + 2 * p, HY, Y0, p)
+    for p in range(X0 // 2):
+        S1[H1 + p, pl.ds(HY, Y0 // 2)] = restricted(0, Y0 // 2, p)
     source1_halo = halo_copies(3, S1, X0 // 2, H1, Y0 // 2, 4, 4, 4)
     start_all(source1_halo)
     land_all(beta1_late)
-    setup(1, B1, CX1, CY1, CM1, CP1, Q1, D1, 1, 17, row1, rows1, H1, X0 // 2, Y0 // 2)
+    setup(1, B1, CX1, CY1, CM1, CP1, Q1, 1, 17, row1, rows1, H1, X0 // 2, Y0 // 2)
 
     for copies in (beta_halo, beta1_halo, beta2_window, source_halo, beta_late[0], beta1_late[0]):
         sent_all(copies)
@@ -613,23 +630,22 @@
         T[x2 + 2, pl.ds(0, 24)] = one
     for x2 in range(-2, 6):
         add = T[x2 + 2, pl.ds(6, 12)]
+        for odd in (0, 1):
+            T[x2 + 14, pl.ds(odd, 12, stride=2)] = add
+    for x2 in range(-2, 6):
         for i in (2 * x2 + 5, 2 * x2 + 6):
             if 2 <= i < 16:
-                for odd in (0, 1):
-                    at = pl.ds(row1 + odd, 12, stride=2)
-                    U1[i, at] = U1[i, at] + add
+                U1[i, pl.ds(row1, rows1)] = U1[i, pl.ds(row1, rows1)] + T[x2 + 14, pl.ds(0, rows1)]
     sweep(1, U1, V1, S1, Q1, coeffs1, 3, 15, row1, rows1)
     sweep(1, V1, U1, S1, Q1, coeffs1, 4, 14, row1, rows1)
 
-    def prolong0(i, carry):
-        add = U1[i + 3, pl.ds(6, 20)]
-        for half in (0, 1):
-            for odd in (0, 1):
-                at = pl.ds(row0 + odd, 20, stride=2)
-                U0[2 * i + half, at] = U0[2 * i + half, at] + add
-        return carry
-
-    lax.fori_loop(1, 11, prolong0, 0, unroll=True)
+    for p in range(1, 11):
+        add = U1[p + 3, pl.ds(6, 20)]
+        for odd in (0, 1):
+            T[p, pl.ds(odd, 20, stride=2)] = add
+    for p in range(1, 11):
+        for i in (2 * p, 2 * p + 1):
+            U0[i, pl.ds(row0, rows0)] = U0[i, pl.ds(row0, rows0)] + T[p, pl.ds(0, rows0)]
     sweep(0, U0, V0, S0, Q0, coeffs0, 3, 21, row0, rows0)
     sweep(0, V0, out_ref, S0, Q0, coeffs0, 4, 20, HY, Y0, H0, HY)
 
@@ -646,10 +662,10 @@
         out_shape=jax.ShapeDtypeStruct(right_side.shape, F32),
         in_specs=[pl.BlockSpec(memory_space=pltpu.HBM)] * 2,
         out_specs=pl.BlockSpec(memory_space=pltpu.VMEM),
-        scratch_shapes=[level0] * 10
-        + [level1] * 10
+        scratch_shapes=[level0] * 9
+        + [level1] * 9
         + [
-            pltpu.VMEM((12, Y0 + 8, LANES), F32),
+            pltpu.VMEM((36, Y0 + 8, LANES), F32),
             level0,
             level1,
             pltpu.VMEM((8, LANES), F32),

time: 23.4 us -> 23 us (0.983)
  Pallas kernels: 22.5 us -> 22.1 us
    pallas_call x1, Pallas kernels: 22.5 us -> 22.1 us  [in_one_kernel(): pl.pallas_call(functools.partial(kernel, G, B), out_shape=jax.ShapeDtypeS...]
where the time goes in v4:
time: 23 us; the launch traced here: 22.8 us
  Pallas kernels  22.1 us (96%)
  local copies, waits for them, and re-layouts  0.71 us (3%)
    pallas_call x1, Pallas kernels, in_one_kernel(): pl.pallas_call(functools.partial(kernel, G, B), out_shape=jax.ShapeDtypeS...  22.1 us
    unnamed x1, local copies, waits for them, and re-layouts  0.71 us

profile of v4, /device:TPU:0, one launch (start us, length us, event | category | flops | bytes accessed | tf_op | source)
XLA Modules:
  0.0 22.8 jit_solution(14528903196679734786)
XLA Ops:
  0.0 22.1 %shard_map.28 = f32[16,32,128]{2,1,0:T(8,128)S(1)} custom-call(f32[16,32,128]{2,1,0:T(8,128)} %rs_ref.1, f32[16,32,128]{2,1,0:T(8,128)} %be_ref.1), custom_call_target="tpu_custom_call" | custom-call | tf_op jit(solution)/shard_map/pallas_call | solution.py:660
  22.1 0.7 %copy.4 = f32[16,32,128]{2,1,0:T(8,128)} copy(f32[16,32,128]{2,1,0:T(8,128)S(1)} %shard_map.28) | data formatting | bytes 524288
